TPU v7x, 128 devices: a whole 4x4x4 slice. The times are simulated.
128 devices in a mesh: cplx: 2 (over core), samp: 32 (over z, y_lo, x), head: 2 (over y_hi).
Axes of the slice: x: 4, y: 4 (y_hi: 2, y_lo: 2; y = y_hi * 2 + y_lo), z: 4, core: 2. Of those that a mesh axis runs over, the one named last changes fastest.
Arguments:
- activations: bfloat16 [2, 32, 256, 768], P('cplx', 'samp'), may hold values from -6 to 6
- conditioning: bfloat16 [2, 256, 384], P('cplx'), may hold values from -6 to 6
- pair: bfloat16 [2, 256, 256, 128], P('cplx', 'samp'), may hold values from -6 to 6
- counts: int32 [2], P('cplx'), may hold values from 128 to 256, as said below
- ada_weight: bfloat16 [2, 384, 1536], replicated, may hold values from -0.3125 to 0.3125
- ada_bias: bfloat16 [2, 768], replicated, may hold values from -4 to 4
- cond_gain: bfloat16 [2, 384], replicated, may hold values from 0.099609375 to 1.8984375
- zero_weight: bfloat16 [2, 384, 768], replicated, may hold values from -0.3125 to 0.3125
- zero_bias: bfloat16 [2, 768], replicated, may hold values from -4 to 4
- qkvg_weight: bfloat16 [768, 4, 768], P(None, None, 'head'), may hold values from -0.21875 to 0.21875
- q_bias: bfloat16 [768], P('head'), may hold values from -3 to 3
- out_weight: bfloat16 [768, 768], P('head'), may hold values from -2.5 to 2.5
- in_weight: bfloat16 [768, 2, 1536], P(None, None, 'head'), may hold values from -0.21875 to 0.21875
- hid_weight: bfloat16 [1536, 768], P('head'), may hold values from -0.15625 to 0.15625
- pair_gain: bfloat16 [128], replicated, may hold values from 0.099609375 to 1.8984375
- bias_weight: bfloat16 [128, 16], P(None, 'head'), may hold values from -0.5 to 0.5
- cotangent: bfloat16 [2, 32, 256, 768], P('cplx', 'samp'), may hold values from -6 to 6
Outputs:
- mixed: bfloat16 [2, 32, 256, 768], P('cplx', 'samp')
- grad_activations: float32 [2, 32, 256, 768], P('cplx', 'samp')
- grad_conditioning: float32 [2, 256, 384], P('cplx')
- grad_pair: float32 [2, 256, 256, 128], P('cplx', 'samp')
- grad_ada_weight: float32 [2, 384, 1536], replicated
- grad_ada_bias: float32 [2, 768], replicated
- grad_cond_gain: float32 [2, 384], replicated
- grad_zero_weight: float32 [2, 384, 768], replicated
- grad_zero_bias: float32 [2, 768], replicated
- grad_qkvg_weight: float32 [768, 4, 768], P(None, None, 'head')
- grad_q_bias: float32 [768], P('head')
- grad_out_weight: float32 [768, 768], P('head')
- grad_in_weight: float32 [768, 2, 1536], P(None, None, 'head')
- grad_hid_weight: float32 [1536, 768], P('head')
- grad_pair_gain: float32 [128], replicated
- grad_bias_weight: float32 [128, 16], P(None, 'head')
Inputs may be any that keep to these rules, and one draw needn't show every extreme that they name: `counts`: one complex uses all 256 positions, the other at least half of them.
All inputs are finite; a program needn't handle non-finite values.
Results may differ from a plain program's by a relative error of at most 0.028.
Values may be sent and summed in bfloat16 or wider, within the bound.
A program may use at most 128 MiB of HBM per device.

v0:
```python
import math

import jax
import jax.numpy as jnp
from jax import lax
from jax.sharding import PartitionSpec as P

D = 768
HD = 48


EPS = 1e-05
HIGH = lax.Precision.HIGHEST


def normalize(tensor):
    row_mean = jnp.mean(tensor, -1, keepdims=True)
    centered = tensor - row_mean
    inv_std = lax.rsqrt(jnp.mean(centered * centered, -1, keepdims=True) + EPS)
    return (centered * inv_std, inv_std)


def norm_back(grad_hat, normed, inv_std):
    return inv_std * (
        grad_hat
        - jnp.mean(grad_hat, -1, keepdims=True)
        - normed * jnp.mean(grad_hat * normed, -1, keepdims=True)
    )


def local(
    activations,
    conditioning,
    pair,
    counts,
    ada_weight,
    ada_bias,
    cond_gain,
    zero_weight,
    zero_bias,
    qkvg_weight,
    q_bias,
    out_weight,
    in_weight,
    hid_weight,
    pair_gain,
    bias_weight,
    cotangent,
):
    act_f = activations[0].astype(jnp.float32)
    samples = act_f.shape[0]
    length = act_f.shape[1]
    local_heads = bias_weight.shape[1]
    local_width = q_bias.shape[0]
    score_scale = 1.0 / math.sqrt(HD)
    single = conditioning[0].astype(jnp.float32)
    ada_float = ada_weight.astype(jnp.float32)
    zero_float = zero_weight.astype(jnp.float32)
    gain_float = cond_gain.astype(jnp.float32)
    single_hat, single_inv = normalize(single)
    scaled = single_hat[None] * gain_float[:, None, :]
    projected = jnp.einsum("wnc,wcd->wnd", scaled, ada_float, precision=HIGH)
    mod_gate = jax.nn.sigmoid(projected[:, :, :D] + ada_bias.astype(jnp.float32)[:, None, :])
    mod_shift = projected[:, :, D:]
    zero_gate = jax.nn.sigmoid(
        jnp.einsum("nc,wcd->wnd", single, zero_float, precision=HIGH)
        + zero_bias.astype(jnp.float32)[:, None, :]
    )
    pair_gain_f = pair_gain.astype(jnp.float32)
    pair_hat, pair_inv = normalize(pair[0].astype(jnp.float32))
    pair_low = (pair_hat * pair_gain_f).astype(jnp.bfloat16)
    bias_part = jnp.einsum(
        "rjp,ph->hrj", pair_low, bias_weight, preferred_element_type=jnp.float32
    ).astype(jnp.bfloat16)
    pair_bias = lax.all_gather(bias_part, "samp", axis=1, tiled=True)
    act_hat, act_inv = normalize(act_f)
    attn_in = (mod_gate[0] * act_hat + mod_shift[0]).astype(jnp.bfloat16)
    trans_in = (mod_gate[1] * act_hat + mod_shift[1]).astype(jnp.bfloat16)
    heads_in = jnp.einsum("snd,dke->ksne", attn_in, qkvg_weight, preferred_element_type=jnp.float32)
    queries = (
        (heads_in[0] + q_bias.astype(jnp.float32))
        .astype(jnp.bfloat16)
        .reshape(samples, length, local_heads, HD)
    )
    key_heads = heads_in[1].astype(jnp.bfloat16).reshape(samples, length, local_heads, HD)
    values = heads_in[2].astype(jnp.bfloat16).reshape(samples, length, local_heads, HD)
    gate_pre = heads_in[3]
    key_valid = lax.broadcasted_iota(jnp.int32, (length,), 0) < counts[0]
    bias_float = pair_bias.astype(jnp.float32)

    def scores_of(q_side, k_side):
        raw_scores = (
            jnp.einsum("sihe,sjhe->shij", q_side, k_side, preferred_element_type=jnp.float32)
            * score_scale
            + bias_float[None]
        )
        return jnp.where(key_valid[None, None, None, :], raw_scores, -1000000000.0)

    scores = scores_of(queries, key_heads)
    row_max = jnp.max(scores, -1, keepdims=True)
    exp_scores = jnp.exp(scores - row_max)
    row_sum = jnp.sum(exp_scores, -1, keepdims=True)
    attn_probs = exp_scores / row_sum
    log_sum = row_max + jnp.log(row_sum)
    probs_low = attn_probs.astype(jnp.bfloat16)
    attended = jnp.einsum(
        "shij,sjhe->sihe", probs_low, values, preferred_element_type=jnp.float32
    ).reshape(samples, length, local_width)
    gate_sig = jax.nn.sigmoid(gate_pre)
    gated_out = (gate_sig * attended).astype(jnp.bfloat16)
    attn_part = jnp.einsum("snf,fd->snd", gated_out, out_weight, preferred_element_type=jnp.float32)
    hidden_in = jnp.einsum("snd,dkf->ksnf", trans_in, in_weight, preferred_element_type=jnp.float32)
    gate_in = hidden_in[0]
    up_in = hidden_in[1]
    gate_in_sig = jax.nn.sigmoid(gate_in)
    silu_val = gate_in * gate_in_sig
    hidden = (silu_val * up_in).astype(jnp.bfloat16)
    trans_part = jnp.einsum("snf,fd->snd", hidden, hid_weight, preferred_element_type=jnp.float32)
    attn_full, trans_full = (
        lax.psum(attn_part.astype(jnp.bfloat16), "head").astype(jnp.float32),
        lax.psum(trans_part.astype(jnp.bfloat16), "head").astype(jnp.float32),
    )
    mixed = (act_f + zero_gate[0] * attn_full + zero_gate[1] * trans_full).astype(jnp.bfloat16)
    grad_out = cotangent[0].astype(jnp.float32)
    grad_attn_out = (zero_gate[0] * grad_out).astype(jnp.bfloat16)
    grad_trans_out = (zero_gate[1] * grad_out).astype(jnp.bfloat16)
    zero_pre = (
        jnp.stack([jnp.sum(grad_out * attn_full, 0), jnp.sum(grad_out * trans_full, 0)])
        * zero_gate
        * (1.0 - zero_gate)
    )
    grad_zero_weight = jnp.einsum("nc,wnd->wcd", single, zero_pre, precision=HIGH)
    grad_zero_bias = jnp.sum(zero_pre, 1)
    grad_out_weight = jnp.einsum(
        "snf,snd->fd", gated_out, grad_attn_out, preferred_element_type=jnp.float32
    )
    grad_gated = jnp.einsum(
        "snd,fd->snf", grad_attn_out, out_weight, preferred_element_type=jnp.float32
    )
    grad_gate_pre = (grad_gated * attended * gate_sig * (1.0 - gate_sig)).astype(jnp.bfloat16)
    grad_attended = (
        (grad_gated * gate_sig).astype(jnp.bfloat16).reshape(samples, length, local_heads, HD)
    )
    probs_back = jnp.exp(scores_of(queries, key_heads) - log_sum)
    grad_probs = jnp.einsum(
        "sihe,sjhe->shij", grad_attended, values, preferred_element_type=jnp.float32
    )
    delta = jnp.sum(probs_back * grad_probs, -1, keepdims=True)
    grad_scores = (probs_back * (grad_probs - delta)).astype(jnp.bfloat16)
    grad_queries = (
        (
            jnp.einsum(
                "shij,sjhe->sihe", grad_scores, key_heads, preferred_element_type=jnp.float32
            )
            * score_scale
        )
        .astype(jnp.bfloat16)
        .reshape(samples, length, local_width)
    )
    grad_keys = (
        (
            jnp.einsum("shij,sihe->sjhe", grad_scores, queries, preferred_element_type=jnp.float32)
            * score_scale
        )
        .astype(jnp.bfloat16)
        .reshape(samples, length, local_width)
    )
    grad_values = (
        jnp.einsum("shij,sihe->sjhe", probs_low, grad_attended, preferred_element_type=jnp.float32)
        .astype(jnp.bfloat16)
        .reshape(samples, length, local_width)
    )
    grad_bias_part = jnp.sum(grad_scores, 0, dtype=jnp.float32)
    grad_heads = jnp.stack([grad_queries, grad_keys, grad_values, grad_gate_pre])
    grad_qkvg_weight = jnp.einsum(
        "snd,ksne->dke", attn_in, grad_heads, preferred_element_type=jnp.float32
    )
    grad_q_bias = jnp.sum(grad_queries, (0, 1), dtype=jnp.float32)
    grad_attn_in = jnp.einsum(
        "ksne,dke->snd", grad_heads, qkvg_weight, preferred_element_type=jnp.float32
    )
    grad_hidden = jnp.einsum(
        "snd,fd->snf", grad_trans_out, hid_weight, preferred_element_type=jnp.float32
    )
    grad_hid_weight = jnp.einsum(
        "snf,snd->fd", hidden, grad_trans_out, preferred_element_type=jnp.float32
    )
    grad_gate_in = grad_hidden * up_in * gate_in_sig * (1.0 + gate_in * (1.0 - gate_in_sig))
    grad_up_in = grad_hidden * silu_val
    grad_ffn = jnp.stack([grad_gate_in, grad_up_in]).astype(jnp.bfloat16)
    grad_in_weight = jnp.einsum(
        "snd,ksnf->dkf", trans_in, grad_ffn, preferred_element_type=jnp.float32
    )
    grad_trans_in = jnp.einsum(
        "ksnf,dkf->snd", grad_ffn, in_weight, preferred_element_type=jnp.float32
    )
    grad_bias = lax.psum_scatter(
        grad_bias_part.astype(jnp.bfloat16), "samp", scatter_dimension=1, tiled=True
    )
    grad_bias_weight = jnp.einsum(
        "rjp,hrj->ph", pair_low, grad_bias, preferred_element_type=jnp.float32
    )
    grad_pair_low = jnp.einsum(
        "hrj,ph->rjp", grad_bias, bias_weight, preferred_element_type=jnp.float32
    )
    grad_attn_in, grad_trans_in, grad_pair_low = (
        lax.psum(grad_attn_in.astype(jnp.bfloat16), "head").astype(jnp.float32),
        lax.psum(grad_trans_in.astype(jnp.bfloat16), "head").astype(jnp.float32),
        lax.psum(grad_pair_low.astype(jnp.bfloat16), "head").astype(jnp.float32),
    )
    grad_pair_gain = jnp.sum(grad_pair_low * pair_hat, (0, 1))
    grad_pair = norm_back(grad_pair_low * pair_gain_f, pair_hat, pair_inv)
    grad_norm_out = jnp.stack([grad_attn_in, grad_trans_in])
    gate_grad = jnp.sum(grad_norm_out * act_hat[None], 1) * mod_gate * (1.0 - mod_gate)
    shift_grad = jnp.sum(grad_norm_out, 1)
    grad_ada_pre = jnp.concatenate([gate_grad, shift_grad], -1)
    grad_ada_weight = jnp.einsum("wnc,wnd->wcd", scaled, grad_ada_pre, precision=HIGH)
    grad_ada_bias = jnp.sum(gate_grad, 1)
    grad_scaled = jnp.einsum("wnd,wcd->wnc", grad_ada_pre, ada_float, precision=HIGH)
    grad_cond_gain = jnp.sum(grad_scaled * single_hat[None], 1)
    grad_single_hat = jnp.sum(grad_scaled * gain_float[:, None, :], 0)
    grad_single = norm_back(grad_single_hat, single_hat, single_inv) + jnp.einsum(
        "wnd,wcd->nc", zero_pre, zero_float, precision=HIGH
    )
    grad_act_hat = mod_gate[0] * grad_attn_in + mod_gate[1] * grad_trans_in
    grad_act = grad_out + norm_back(grad_act_hat, act_hat, act_inv)
    summed = lax.psum(
        (
            grad_ada_weight,
            grad_ada_bias,
            grad_cond_gain,
            grad_zero_weight,
            grad_zero_bias,
            grad_qkvg_weight,
            grad_q_bias,
            grad_out_weight,
            grad_in_weight,
            grad_hid_weight,
            grad_pair_gain,
            grad_bias_weight,
        ),
        ("cplx", "samp"),
    )
    grad_single = lax.psum(grad_single.astype(jnp.bfloat16), "samp").astype(jnp.float32)
    return (
        mixed[None],
        grad_act[None],
        grad_single[None],
        grad_pair[None],
        summed[0],
        summed[1],
        summed[2],
        summed[3],
        summed[4],
        summed[5],
        summed[6],
        summed[7],
        summed[8],
        summed[9],
        summed[10],
        summed[11],
    )


def solution(mesh):
    placed = (
        P("cplx", "samp", None, None),
        P("cplx", None, None),
        P("cplx", "samp", None, None),
        P("cplx"),
        P(),
        P(),
        P(),
        P(),
        P(),
        P(None, None, "head"),
        P("head"),
        P("head", None),
        P(None, None, "head"),
        P("head", None),
        P(),
        P(None, "head"),
        P("cplx", "samp", None, None),
    )
    return jax.shard_map(
        local,
        mesh=mesh,
        in_specs=placed,
        out_specs=(
            P("cplx", "samp", None, None),
            P("cplx", "samp", None, None),
            P("cplx", None, None),
            P("cplx", "samp", None, None),
            P(),
            P(),
            P(),
            P(),
            P(),
            P(None, None, "head"),
            P("head"),
            P("head", None),
            P(None, None, "head"),
            P("head", None),
            P(),
            P(None, "head"),
        ),
        check_vma=False,
    )
```

profile of v0, /device:TPU:1, one launch (start us, length us, event | category | flops | bytes accessed | tf_op | source)
XLA Modules:
  0.0 1402.1 jit_solution(1187158984699882956)
XLA Ops:
  11.1 2.4 fusion.55
  14.6 4.5 fusion.53
  22.1 1.9 fusion.164
  27.1 2.0 divide_bitcast_fusion
  29.1 2.4 fusion.122
  35.4 2.7 fusion.21
  42.3 104.2 %all-gather.2.cloned.1.call-done = bf16[8,256,256]{2,0,1:T(8,128)(2,1)} async-done(((bf16[8,8,256]{2,0,1:T(8,128)(2,1)}), bf16[8,256,256]{2,0,1:T(8,128)(2,1)}) %all-gather.2.cloned.1.call-update) | async-done | bytes 1048592 | tf_op jit(solution)/shard_map/all_gather | solution.py:75
  153.3 1.8 copy.109
  155.5 3.2 fusion.40
  159.8 1.9 copy.97
  161.7 2.4 convolution_convert_fusion.3
  165.9 2.1 fusion.49
  169.7 2.5 convert_reduce_fusion.3
  173.4 2.6 fusion.39
  179.4 132.6 %reduce-scatter.2.cloned.1.call-done = bf16[8,8,256]{2,0,1:T(8,128)(2,1)} async-done(((bf16[8,256,256]{2,0,1:T(8,128)(2,1)}), bf16[8,8,256]{2,0,1:T(8,128)(2,1)}) %reduce-scatter.2.cloned.1.call-update) | async-done | bytes 32784 | tf_op jit(solution)/shard_map/reduce_scatter | solution.py:197
  312.1 1.9 convolution_convert_fusion
  315.8 3.6 fusion.118
  319.3 3.0 fusion.99
  323.7 3.0 fusion.136
  326.7 82.2 %all-reduce.11.cloned.1.call-done = (bf16[1,256,768]{2,1,0:T(8,128)(2,1)}, bf16[1,256,768]{2,1,0:T(8,128)(2,1)}, bf16[1,256,768]{2,1,0:T(8,128)(2,1)}, bf16[1,256,768]{2,1,0:T(8,128)(2,1)}, bf16[8,256,128]{2,1,0:T(8,128)(2,1)}) async-done(((bf16[1,256,768]{2,1,0:T(8,128)(2,1)}, bf16[1,256,768]{2,1,0:T(8,128)(2,1)}, bf16[1,256,768]{2,1,0:T(8,128)(2,1)}, bf16[1,256,768]{2,1,0:T(8,128)(2,1)}, ...) | async-done | bytes 2097168 | tf_op jit(solution)/shard_map/psum | solution.py:121
  414.6 3.3 multiply_reduce_fusion.2
  417.9 5.7 fusion
  425.4 2.1 fusion.51
  427.8 2.8 convolution_bitcast_fusion
  433.2 2.4 fusion.67
  436.2 283.3 %all-reduce = (f32[2,768]{1,0:T(2,128)}, f32[2,384]{1,0:T(2,128)}, f32[2,768]{1,0:T(2,128)}, f32[384]{0:T(512)}, f32[128]{0:T(128)}, /*index=5*/f32[128,8]{0,1:T(8,128)}) all-reduce(f32[2,768]{1,0:T(2,128)S(1)} %copy-done.65, f32[2,384]{1,0:T(2,128)S(1)} %copy-done.71, ...), channel_id=1, replica_groups=mesh['cplx'=2,'samp'=32,'head'=2] {'cplx','samp'}, use_global_device_ids=true, to_apply=%region_25.26 | all-reduce | flops 5376 | bytes 43008 | tf_op jit(solution)/shard_map/psum | solution.py:227
  719.5 3.1 fusion.64
  724.3 648.7 %all-reduce.9.cloned.1.call-done = (f32[2,384,1536]{2,1,0:T(8,128)}, f32[2,384,768]{1,2,0:T(8,128)}, f32[768,4,384]{2,0,1:T(8,128)}, f32[384,768]{1,0:T(8,128)},...) async-done(((f32[2,384,1536]{2,1,0:T(8,128)}, f32[2,384,768]{1,2,0:T(8,128)}, f32[768,4,384]{2,0,1:T(8,128)}, f32[384,768]{1,0:T(8,128)}, f32[768,2,768]{2,0,1:T(8,128)}, ...) | async-done | bytes 20054032 | tf_op jit(solution)/shard_map/psum | solution.py:227
  1373.0 3.1 copy.115
  1376.1 7.7 copy.116
  1383.8 5.8 copy.117
  1389.7 2.2 copy.167
  (243 shorter events, 53.4 us)
Async XLA Ops:
  7.2 14.9 %copy-start = (bf16[768,4,384]{2,1,0:T(4,128)(2,1)S(1)}, bf16[768,4,384]{2,1,0:T(4,128)(2,1)}, u32[]{:S(2)}) copy-start(bf16[768,4,384]{2,1,0:T(4,128)(2,1)} %param.26) | copy-start | bytes 7077892
  7.2 6.4 copy-start.9
  7.2 6.8 copy-start.12
  7.2 139.3 %all-gather.2.cloned.1.call-start = ((), (), s32[]{:S(2)}) async-start(), calls=%async_computation.1 | async-start | bytes 1081344 | tf_op jit(solution)/shard_map/all_gather | solution.py:75
  8.1 6.1 copy-start.72
  9.4 5.0 copy-start.75
  9.4 5.0 copy-start.69
  13.5 298.6 %reduce-scatter.2.cloned.1.call-start = ((), (), s32[]{:S(2)}) async-start(), calls=%async_computation.3 | async-start | bytes 1081344 | tf_op jit(solution)/shard_map/reduce_scatter | solution.py:197
  13.7 5.8 copy-start.56
  14.0 5.6 copy-start.62
  14.2 4.9 copy-start.60
  42.3 105.9 %copy-start.55 = (f32[8,48]{1,0:T(8,128)S(1)}, f32[8,48]{1,0:T(8,128)}, u32[]{:S(2)}) copy-start(f32[8,48]{1,0:T(8,128)} %reshape.620) | copy-start | bytes 4612
  155.1 253.8 %all-reduce.11.cloned.1.call-start = ((), (), s32[]{:S(2)}) async-start(), calls=%async_computation.5 | async-start | bytes 4194304 | tf_op jit(solution)/shard_map/psum | solution.py:121
  177.8 134.2 %copy-start.74 = (bf16[128,8]{0,1:T(8,128)(2,1)S(1)}, bf16[128,8]{0,1:T(8,128)(2,1)}, u32[]{:S(2)}) copy-start(bf16[128,8]{0,1:T(8,128)(2,1)} %param.32) | copy-start | bytes 6148
  179.4 134.6 %copy-start.10 = (bf16[1,1,256,768]{3,2,1,0:T(8,128)(2,1)S(1)}, bf16[1,1,256,768]{3,2,1,0:T(8,128)(2,1)}, u32[]{:S(2)}) copy-start(bf16[1,1,256,768]{3,2,1,0:T(8,128)(2,1)} %param.17) | copy-start | bytes 1179652
  179.4 134.7 %copy-start.57 = (f32[256]{0:T(256)S(1)}, f32[256]{0:T(256)}, u32[]{:S(2)}) copy-start(f32[256]{0:T(256)} %copy-done.56) | copy-start | bytes 3076
  179.4 134.7 %copy-start.63 = (f32[256]{0:T(256)S(1)}, f32[256]{0:T(256)}, u32[]{:S(2)}) copy-start(f32[256]{0:T(256)} %copy-done.62) | copy-start | bytes 3076
  314.0 408.6 %all-reduce.7.cloned.1.call-start = ((), (), s32[]{:S(2)}) async-start(), calls=%async_computation.2 | async-start | bytes 393216 | tf_op jit(solution)/shard_map/psum | solution.py:244
  323.7 85.2 %copy-start.8 = (f32[2,256,768]{2,1,0:T(8,128)S(1)}, f32[2,256,768]{2,1,0:T(8,128)}, u32[]{:S(2)}) copy-start(f32[2,256,768]{2,1,0:T(8,128)} %copy-done.7) | copy-start | bytes 4718596
  417.9 5.7 copy-start.13
  417.9 5.7 copy-start.61
  417.9 5.7 copy-start.67
  417.9 6.0 copy-start.27
  417.9 6.0 copy-start.48
  417.9 6.0 copy-start.49
  417.9 6.0 copy-start.58
  417.9 6.0 copy-start.64
  427.5 945.4 %all-reduce.9.cloned.1.call-start = ((), (), s32[]{:S(2)}) async-start(), calls=%async_computation.4 | async-start | bytes 40108032 | tf_op jit(solution)/shard_map/psum | solution.py:227
  1373.0 10.8 slice-start.2
  1376.1 7.7 slice-start.3
  1383.8 5.8 slice-start
  1383.8 5.8 slice-start.1
  (58 other events, 130.8 us)
Sparse Core Ops, SparseCore 0:
  13.6 132.8 all-gather.1
  155.2 156.8 reduce-scatter.1
  315.7 93.1 all-reduce.10
  427.7 272.9 all-reduce.6
  705.0 667.9 all-reduce.8
where the time goes:
time: 1410 us; the launch traced here: 1400 us
  waiting for transfers between devices  968 us (69%)
  blocking collectives  283 us (20%)
  matrix products  64.5 us (5%)
  local copies, waits for them, and re-layouts  46.2 us (3%)
  other arithmetic  24 us (2%)
  between operations  15.5 us (1%)
    psum x1, waiting for transfers between devices, local(): lax.psum((grad_ada_weight, grad_ada_bias, grad_cond_gain, grad_zero_weigh...  649 us
    psum x1, blocking collectives, local(): lax.psum((grad_ada_weight, grad_ada_bias, grad_cond_gain, grad_zero_weigh...  283 us
    reduce_scatter x1, waiting for transfers between devices, local(): lax.psum_scatter(grad_bias_part.astype(jnp.bfloat16), 'samp', scatter_dim...  133 us
    all_gather x1, waiting for transfers between devices, local(): pair_bias = lax.all_gather(bias_part, 'samp', axis=1, tiled=True)  104 us
    psum x1, waiting for transfers between devices, local(): lax.psum(trans_part.astype(jnp.bfloat16), 'head').astype(jnp.float32)  82.2 us
    unnamed x176, local copies, waits for them, and re-layouts  31.2 us
  transfers between devices with their start and end apart: 5, of which 4 were waited for; matrix products, arithmetic and copies ran while one was open for 5% of the time, Pallas kernels for 0%

commit v1 on v0

v1 whole, which is shorter than its diff:
```python
import functools
import math

import jax
import jax.numpy as jnp
from jax import lax
from jax.experimental import pallas as pl
from jax.experimental.pallas import tpu as pltpu
from jax.sharding import PartitionSpec as P

D = 768
HD = 48
EPS = 1e-05
HIGH = lax.Precision.HIGHEST
MESH = pl.DeviceIdType.MESH
BF = jnp.bfloat16
F32 = jnp.float32
NS = 32
VMEM = pltpu.VMEM


def place():
    samp = lax.axis_index("samp")
    return {
        "c": lax.axis_index("cplx"),
        "h": lax.axis_index("head"),
        "s": samp,
        "z": samp // 8,
        "l": (samp // 4) % 2,
        "x": samp % 4,
        "y": lax.axis_index("head") * 2 + (samp // 4) % 2,
    }


SIZE = {"z": 4, "x": 4, "y": 4, "l": 2}


def peer_on(at, axis, step):
    z, x, lo, hd = at["z"], at["x"], at["l"], at["h"]
    q = (at[axis] + step) % SIZE[axis]
    if axis == "z":
        z = q
    elif axis == "x":
        x = q
    elif axis == "l":
        lo = q
    else:
        hd, lo = q // 2, q % 2
    return {"cplx": at["c"], "samp": z * 8 + lo * 4 + x, "head": hd}, q


def signal(bar, dev):
    pl.semaphore_signal(bar, inc=1, device_id=dev, device_id_type=MESH)


def samp_dev(at, other):
    return {"cplx": at["c"], "samp": other, "head": at["h"]}


def head_dev(at):
    return {"cplx": at["c"], "samp": at["s"], "head": 1 - at["h"]}


def core_dev(at):
    return {"cplx": 1 - at["c"], "samp": at["s"], "head": at["h"]}


def rcopy(src, dst, send, recv, dev):
    return pltpu.make_async_remote_copy(
        src_ref=src, dst_ref=dst, send_sem=send, recv_sem=recv, device_id=dev, device_id_type=MESH
    )


def greet_samp(at, bar):
    def one(i, _):
        signal(bar, samp_dev(at, (at["s"] + i) % NS))
        return 0

    lax.fori_loop(1, NS, one, 0)


SCALE = 1.0 / math.sqrt(HD)


def dot(a, b):
    return lax.dot_general(a, b, (((1,), (0,)), ((), ())), preferred_element_type=F32)


def dot_t(a, b):
    return lax.dot_general(a, b, (((1,), (1,)), ((), ())), preferred_element_type=F32)


def dot_l(a, b):
    return lax.dot_general(a, b, (((0,), (0,)), ((), ())), preferred_element_type=F32)


def mean(v):
    return jnp.mean(v, -1, keepdims=True)


def normalize(tensor):
    centered = tensor - mean(tensor)
    inv_std = lax.rsqrt(mean(centered * centered) + EPS)
    return (centered * inv_std, inv_std)


def norm_back(grad_hat, normed, inv_std):
    return inv_std * (grad_hat - mean(grad_hat) - normed * mean(grad_hat * normed))


def sigmoid(v):
    return 1.0 / (1.0 + jnp.exp(-v))


def flip(v):
    return v.astype(F32).T.astype(BF)


def loop(count, body):
    def step(i, _):
        body(i)
        return 0

    lax.fori_loop(0, count, step, 0)


def put(ref, start, value):
    rows, cols = value.shape
    n = rows // 16
    for j in range(cols // 128):
        ref[pl.ds(start + j * n, n)] = (
            value[:, j * 128 : (j + 1) * 128].astype(BF).reshape(n, 16, 128)
        )


TILES = (832, 384, 768, 512, 64)
HALF = (416, 192, 384, 256, 64)
GROUPS = (
    (0, 0, 192, "zxl"),
    (0, 192, 224, "xzl"),
    (1, 0, 128, "yzx"),
    (1, 128, 64, "zyx"),
    (2, 0, 192, "zxl"),
    (2, 192, 192, "xzl"),
    (3, 0, 192, "yxz"),
    (3, 192, 64, "xyz"),
    (4, 0, 64, "yzx"),
)
FIRST = (0, 1, 2, 3)
SECOND = (4, 5, 6, 7, 8)
T_IN, T_HID = 0, 576
T_ADA, T_ZERO = (0, 0), (288, 288)
T_QKVG, T_OUT, T_HID2, T_WPAD = 0, 576, 720, 752
T_ZERO2, T_SMALL, T_APAD = 432, 480, 482

INPUTS = (
    ("pair", (8, 256, 128)),
    ("pgain", (128,)),
    ("wt", (8, 128)),
    ("single", (256, 384)),
    ("gain", (2, 384)),
    ("ada", (2, 384, 1536)),
    ("adab", (2, 768)),
    ("zero", (2, 384, 768)),
    ("zerob", (2, 768)),
    ("act", (256, 768)),
    ("cot", (256, 768)),
    ("win", (2, 768, 768)),
    ("hid", (768, 768)),
    ("wq", (4, 768, 384)),
    ("qb", (384,)),
    ("wout", (384, 768)),
)
N = 256
SCRATCH = (
    ("rows", (8, 8, N), F32),
    ("part", (64, N), BF),
    ("bias", (NS, 64, N), BF),
    ("wall", (2, 16, 128), BF),
    ("shat", (N, 384), F32),
    ("sinv", (N, 128), F32),
    ("s_hi", (2, N, 384), BF),
    ("s_lo", (2, N, 384), BF),
    ("s_t", (2, 384, N), BF),
    ("one_t", (384, N), BF),
    ("mg", (2, N, D), F32),
    ("ms", (2, N, D), F32),
    ("zg", (2, N, D), F32),
    ("hat", (N, D), F32),
    ("ain", (N, D), BF),
    ("tin", (N, D), BF),
    ("gao", (N, D), BF),
    ("gto", (N, D), BF),
    ("hidden", (N, D), BF),
    ("ffn", (N, 2 * D), BF),
    ("pre", (N, 2 * D), BF),
    ("zp", (N, D), BF),
    ("mixf", (N, D), F32),
    ("actf", (N, D), F32),
    ("mixs", (N, D), BF),
    ("mixr", (N, D), BF),
    ("acts", (N, D), BF),
    ("actr", (N, D), BF),
    ("gsh", (N, 384), F32),
    ("zterm", (N, 384), F32),
    ("qkv", (3, N, 384), BF),
    ("gsig", (N, 384), F32),
    ("ggat", (N, 384), F32),
    ("gatt", (N, 384), BF),
    ("acc", (4, N, 384), F32),
    ("gheads", (N, 1536), BF),
    ("flipped", (D, N), BF),
    ("held", (NS, 8, N), F32),
    ("small_a", (32, 128), F32),
    ("small_w", (16, 128), F32),
    ("gb", (2, NS, 32, N), BF),
    ("gb1", (2, 3, 8, 32, N), BF),
    ("gb2", (2, 7, 32, N), BF),
    ("gball", (2, 64, N), BF),
    ("gpair", (8, N, 128), F32),
    ("slot", (4, 4, 16, 128), F32),
)
SEMS = (
    ("ld", (len(INPUTS),)),
    ("bs", (NS,)),
    ("br", (NS,)),
    ("hs", (4,)),
    ("hr", (4,)),
    ("cs", (5,)),
    ("cr", (5,)),
    ("rs", (len(GROUPS), 3, 3)),
    ("rr", (len(GROUPS), 3, 3)),
    ("gs", (len(GROUPS), 3, 3)),
    ("gr", (len(GROUPS), 3, 3)),
    ("fs", (len(GROUPS),)),
    ("fr", (len(GROUPS),)),
    ("b1s", (2, 3)),
    ("b1r", (2, 3)),
    ("b2s", (2, 7)),
    ("b2r", (2, 7)),
    ("ss", (4, 3)),
    ("sr", (4, 3)),
    ("out", (12,)),
)
OUTPUTS = tuple(("sum%d" % i, (t, 16, 128), BF) for i, t in enumerate(TILES)) + (
    ("small_o", (16, 128), F32),
    ("mixed_o", (N, D), BF),
    ("act_o", (N, D), F32),
    ("pair_o", (8, N, 128), F32),
)


class Refs:
    pass


def recv_shapes():
    shapes = []
    for g, (_, _, tiles, axes) in enumerate(GROUPS):
        for s, axis in enumerate(axes):
            tiles //= SIZE[axis]
            shapes.append(((g, s), (SIZE[axis] - 1, tiles, 16, 128)))
    return shapes


class Sums:
    def __init__(self, r, at):
        self.r, self.at = r, at
        core = at["c"]
        self.shift = [core * HALF[b] if b < 4 else 0 for b in range(5)]
        self.base = [None] * len(GROUPS)
        self.part = [None] * len(GROUPS)
        self.pending = [None] * len(GROUPS)
        self.pairs = {}
        self.last = {}

    def core_start(self, buf):
        r, at, half = self.r, self.at, HALF[buf]
        cp = rcopy(
            r.tiles[buf].at[pl.ds((1 - at["c"]) * half, half)],
            r.sums[buf].at[pl.ds((1 - at["c"]) * half, half)],
            r.cs.at[buf],
            r.cr.at[buf],
            core_dev(at),
        )
        cp.start()
        self.pairs[buf] = cp

    def core_end(self, buf):
        r, half, start = self.r, HALF[buf], self.shift[buf]
        self.pairs[buf].wait()

        def add(j):
            rows = pl.ds(start + j * 16, 16)
            r.tiles[buf][rows] = (
                r.tiles[buf][rows].astype(F32) + r.sums[buf][rows].astype(F32)
            ).astype(BF)

        loop(half // 16, add)

    def rs_start(self, g, stage):
        r, at = self.r, self.at
        buf, start, tiles, axes = GROUPS[g]
        axis = axes[stage]
        count = SIZE[axis]
        for a in axes[:stage]:
            tiles //= SIZE[a]
        if stage == 0:
            self.base[g] = self.shift[buf] + start
        part = tiles // count
        cps = []
        for i in range(1, count):
            dev, q = peer_on(at, axis, i)
            cp = rcopy(
                r.tiles[buf].at[pl.ds(self.base[g] + q * part, part)],
                r.recv[g, stage].at[i - 1],
                r.rs.at[g, stage, i - 1],
                r.rr.at[g, stage, i - 1],
                dev,
            )
            cp.start()
            cps.append(cp)
        self.pending[g] = cps
        self.part[g] = part

    def rs_end(self, g, stage):
        r = self.r
        buf, _, _, axes = GROUPS[g]
        part = self.part[g]
        for cp in self.pending[g]:
            cp.wait()
        here = self.base[g] + self.at[axes[stage]] * part
        block = max(b for b in range(1, 17) if part % b == 0)

        def add(i):
            rows = pl.ds(i * block, block)
            mine = pl.ds(here + i * block, block)
            total = r.tiles[buf][mine].astype(F32)
            for j in range(SIZE[axes[stage]] - 1):
                total = total + r.recv[g, stage][j, rows].astype(F32)
            to = r.sums if stage == 2 else r.tiles
            to[buf][mine] = total.astype(BF)

        loop(part // block, add)
        self.base[g] = here

    def ag_start(self, g, stage):
        r = self.r
        buf, _, _, axes = GROUPS[g]
        rows = pl.ds(self.base[g], self.part[g])
        cps = []
        for i in range(1, SIZE[axes[stage]]):
            dev, _ = peer_on(self.at, axes[stage], i)
            cp = rcopy(
                r.sums[buf].at[rows],
                r.sums[buf].at[rows],
                r.gs.at[g, stage, i - 1],
                r.gr.at[g, stage, i - 1],
                dev,
            )
            cp.start()
            cps.append(cp)
        self.pending[g] = cps

    def ag_end(self, g, stage):
        axis = GROUPS[g][3][stage]
        for cp in self.pending[g]:
            cp.wait()
        self.base[g] = self.base[g] - self.at[axis] * self.part[g]
        self.part[g] = self.part[g] * SIZE[axis]

    def share_start(self, g):
        r = self.r
        buf, start, tiles, _ = GROUPS[g]
        if buf < 4:
            rows = pl.ds(self.shift[buf] + start, tiles)
            cp = rcopy(
                r.sums[buf].at[rows], r.sums[buf].at[rows], r.fs.at[g], r.fr.at[g], core_dev(self.at)
            )
            cp.start()
            self.last[g] = cp

    def share_end(self, g):
        if g in self.last:
            self.last[g].wait()


def mega_kernel(*refs):
    r = Refs()
    refs = list(refs)

    def take(count):
        got = refs[:count]
        del refs[:count]
        return got

    counts_ref = take(1)[0]
    hbm = take(len(INPUTS))
    outs = dict(zip([o[0] for o in OUTPUTS], take(len(OUTPUTS))))
    for (name, _), ref in zip(INPUTS, take(len(INPUTS))):
        setattr(r, name, ref)
    for (name, _, _), ref in zip(SCRATCH, take(len(SCRATCH))):
        setattr(r, name, ref)
    r.tiles = take(5)
    r.sums = take(5)
    r.recv = {}
    for (key, _), ref in zip(recv_shapes(), take(len(recv_shapes()))):
        r.recv[key] = ref
    for (name, _), ref in zip(SEMS, take(len(SEMS))):
        setattr(r, name, ref)

    at = place()
    me, hd = at["s"], at["h"]
    blocks = [slice(i * 256, (i + 1) * 256) for i in range(3)]
    loads = {}
    for i, (name, _) in enumerate(INPUTS):
        cp = pltpu.make_async_copy(hbm[i], getattr(r, name), r.ld.at[i])
        cp.start()
        loads[name] = cp

    def need(*names):
        for name in names:
            loads[name].wait()

    copies = []

    def leave(src, name):
        cp = pltpu.make_async_copy(src, outs[name], r.out.at[len(copies)])
        cp.start()
        copies.append(cp)

    need("pair", "pgain", "wt")
    pgain = r.pgain[...].astype(F32).reshape(1, 128)
    wt = r.wt[...]
    r.wall[hd] = jnp.concatenate([wt.astype(F32), jnp.zeros((8, 128), F32)], 0).astype(BF)
    for i in range(8):
        normed, _ = normalize(r.pair[i].astype(F32))
        r.rows[:, i, :] = dot_t(wt, (normed * pgain).astype(BF))
    r.part[...] = r.rows[...].reshape(64, N).astype(BF)
    r.bias[me] = r.part[...]
    bar = pltpu.get_barrier_semaphore()
    greet_samp(at, bar)
    cross = {"cplx": at["c"], "samp": at["z"] * 8 + (1 - at["l"]) * 4 + at["x"], "head": 1 - hd}
    for dev in (head_dev(at), core_dev(at), cross):
        signal(bar, dev)
    pl.semaphore_wait(bar, NS + 2)

    def bias_copy(i):
        return rcopy(
            r.part, r.bias.at[me], r.bs.at[i], r.br.at[i], samp_dev(at, (me + i) % NS)
        )

    loop(NS - 1, lambda i: bias_copy(i + 1).start())
    wt_copy = rcopy(r.wall.at[hd], r.wall.at[hd], r.hs.at[0], r.hr.at[0], head_dev(at))
    wt_copy.start()

    r.small_a[...] = jnp.zeros(r.small_a.shape, F32)
    r.small_w[...] = jnp.zeros(r.small_w.shape, F32)
    need("single", "gain")
    gains = r.gain[...].astype(F32)

    def cond(i):
        rows = pl.ds(i * 32, 32)
        normed, inv = normalize(r.single[rows].astype(F32))
        r.shat[rows] = normed
        r.sinv[rows] = jnp.broadcast_to(inv, (32, 128))
        for w in range(2):
            scaled = normed * gains[w : w + 1]
            high = scaled.astype(BF)
            r.s_hi[w, rows] = high
            r.s_lo[w, rows] = (scaled - high.astype(F32)).astype(BF)

    loop(N // 32, cond)
    for w in range(2):
        r.s_t[w] = flip(r.s_hi[w])
    r.one_t[...] = flip(r.single[...])
    need("ada", "adab", "zero", "zerob")
    adab = r.adab[...].astype(F32)
    zerob = r.zerob[...].astype(F32)
    for w in range(2):
        for b in blocks:
            later = slice(D + b.start, D + b.stop)
            pre_gate = dot(r.s_hi[w], r.ada[w, :, b]) + dot(r.s_lo[w], r.ada[w, :, b])
            r.mg[w, :, b] = sigmoid(pre_gate + adab[w : w + 1, b])
            r.ms[w, :, b] = dot(r.s_hi[w], r.ada[w, :, later]) + dot(r.s_lo[w], r.ada[w, :, later])
            r.zg[w, :, b] = sigmoid(dot(r.single[...], r.zero[w, :, b]) + zerob[w : w + 1, b])
    need("act", "cot")

    def norm_in(i):
        rows = pl.ds(i * 16, 16)
        normed, _ = normalize(r.act[rows].astype(F32))
        r.hat[rows] = normed
        r.ain[rows] = (r.mg[0, rows] * normed + r.ms[0, rows]).astype(BF)
        r.tin[rows] = (r.mg[1, rows] * normed + r.ms[1, rows]).astype(BF)
        g = r.cot[rows].astype(F32)
        r.gao[rows] = (r.zg[0, rows] * g).astype(BF)
        r.gto[rows] = (r.zg[1, rows] * g).astype(BF)

    loop(N // 16, norm_in)

    def branch_out(w, b, part):
        gate = r.zg[w, :, b]
        share = gate * part
        r.mixf[:, b] = share if w == 1 else r.mixf[:, b] + share
        grad = r.cot[:, b].astype(F32) * share * (1.0 - gate)
        r.zp[:, b] = grad.astype(BF)
        for j in range(2):
            row = 12 + 6 * w + b.start // 128 + j
            r.small_a[row : row + 1] = jnp.sum(grad[:, j * 128 : (j + 1) * 128], 0, keepdims=True)

    def branch_in(w, b, grad_in):
        gate = r.mg[w, :, b]
        share = gate * grad_in
        r.actf[:, b] = share if w == 1 else r.actf[:, b] + share
        grad = share * r.hat[:, b] * (1.0 - gate)
        r.pre[:, b] = grad.astype(BF)
        r.pre[:, D + b.start : D + b.stop] = grad_in.astype(BF)
        for j in range(2):
            row = 6 * w + b.start // 128 + j
            r.small_a[row : row + 1] = jnp.sum(grad[:, j * 128 : (j + 1) * 128], 0, keepdims=True)

    def conditioned(w, to):
        for i in range(6):
            put(to, T_ADA[w] + i * 48, dot(r.s_t[w], r.pre[:, i * 256 : (i + 1) * 256]))
        for i, b in enumerate(blocks):
            value = dot(r.one_t[...], r.zp[:, b])
            if w == 1 and i == 2:
                put(r.tiles[3], T_ZERO2, value)
            else:
                put(to, T_ZERO[w] + i * 48, value)

    def conditioning_back(w):
        for j in range(3):
            b = slice(j * 128, (j + 1) * 128)
            scaled = dot_t(r.pre[...], r.ada[w, b, :])
            row = 24 + 3 * w + j
            r.small_a[row : row + 1] = jnp.sum(scaled * r.shat[:, b], 0, keepdims=True)
            share = scaled * gains[w : w + 1, b]
            through = dot_t(r.zp[...], r.zero[w, b, :])
            r.gsh[:, b] = share if w == 1 else r.gsh[:, b] + share
            r.zterm[:, b] = through if w == 1 else r.zterm[:, b] + through

    need("win", "hid")
    for b in blocks:
        gate_in = dot(r.tin[...], r.win[0, :, b])
        up_in = dot(r.tin[...], r.win[1, :, b])
        grad_hidden = dot_t(r.gto[...], r.hid[b, :])
        sig = sigmoid(gate_in)
        silu = gate_in * sig
        r.hidden[:, b] = (silu * up_in).astype(BF)
        r.ffn[:, b] = (grad_hidden * up_in * sig * (1.0 + gate_in * (1.0 - sig))).astype(BF)
        r.ffn[:, D + b.start : D + b.stop] = (grad_hidden * silu).astype(BF)
    sums = Sums(r, at)
    r.flipped[...] = flip(r.hidden[...])
    for i, b in enumerate(blocks):
        value = dot(r.flipped[...], r.gto[:, b])
        if i < 2:
            put(r.tiles[0], T_HID + i * 96, value)
        else:
            put(r.tiles[0], T_HID + 192, value[:, :128])
            put(r.tiles[0], T_HID + 240, value[:256, 128:])
            put(r.tiles[2], T_HID2, value[256:, 128:])
    r.flipped[...] = flip(r.tin[...])
    for i in range(6):
        put(r.tiles[0], T_IN + i * 96, dot(r.flipped[...], r.ffn[:, i * 256 : (i + 1) * 256]))
    sums.core_start(0)
    for b in blocks:
        branch_out(1, b, dot(r.hidden[...], r.hid[:, b]))
    for b in blocks:
        branch_in(
            1, b, dot_t(r.ffn[:, :D], r.win[0, b, :]) + dot_t(r.ffn[:, D:], r.win[1, b, :])
        )
    conditioned(1, r.tiles[1])
    sums.core_start(1)
    sums.core_end(0)
    sums.rs_start(0, 0)
    sums.rs_start(1, 0)
    conditioning_back(1)

    need("wq", "qb", "wout")
    r.qkv[0] = (dot(r.ain[...], r.wq[0]) + r.qb[...].astype(F32).reshape(1, 384)).astype(BF)
    r.qkv[1] = dot(r.ain[...], r.wq[1]).astype(BF)
    r.qkv[2] = dot(r.ain[...], r.wq[2]).astype(BF)
    r.gsig[...] = sigmoid(dot(r.ain[...], r.wq[3]))
    r.ggat[...] = dot_t(r.gao[...], r.wout[...])
    r.gatt[...] = (r.ggat[...] * r.gsig[...]).astype(BF)
    sums.core_end(1)
    sums.rs_start(2, 0)
    sums.rs_start(3, 0)
    loop(NS - 1, lambda i: bias_copy(i + 1).wait())
    wt_copy.wait()
    r.acc[...] = jnp.zeros(r.acc.shape, F32)
    lane = lax.broadcasted_iota(jnp.int32, (1, 256), 1)
    mask = jnp.where(lane < counts_ref[0], 0.0, -1e9)
    for h in range(8):
        lo = 0 if h < 5 else 128
        win = slice(lo, lo + 256)
        first = h * HD - lo
        mine = (lane >= first) & (lane < first + HD)
        pick = jnp.where(mine, 1.0, 0.0).astype(BF)
        q_m = r.qkv[0, :, win] * pick
        k_m = r.qkv[1, :, win] * pick
        v_m = r.qkv[2, :, win] * pick
        g_m = r.gatt[:, win] * pick
        pair_rows = r.bias[:, (h // 2) * 16 : (h // 2) * 16 + 16, :].astype(F32)
        bias = pair_rows[:, (h % 2) * 8 : (h % 2) * 8 + 8, :].reshape(N, N)
        scores = dot_t(q_m, r.qkv[1, :, win]) * SCALE + bias + mask
        top = jnp.max(scores, -1, keepdims=True)
        weights = jnp.exp(scores - top)
        probs = weights * (1.0 / jnp.sum(weights, -1, keepdims=True))
        low = probs.astype(BF)
        r.acc[0, :, win] += dot(low, v_m)
        grad_probs = dot_t(g_m, r.qkv[2, :, win])
        delta = jnp.sum(probs * grad_probs, -1, keepdims=True)
        grad_s = probs * (grad_probs - delta)
        grad_low = grad_s.astype(BF)
        r.acc[1, :, win] += dot(grad_low, k_m)
        r.acc[2, :, win] += dot_l(grad_low, q_m)
        r.acc[3, :, win] += dot_l(low, g_m)
        split = grad_s.reshape(NS, 8, N)
        if h % 2 == 0:
            r.held[...] = split
        else:
            two = jnp.concatenate([r.held[...], split], 1).astype(BF)
            rows = slice((h // 2 % 2) * 16, (h // 2 % 2) * 16 + 16)
            if h < 4:
                r.gb[0, :, rows, :] = two
            else:
                for s in range(NS):
                    r.gb[1, s % 4 * 8 + s // 8 * 2 + s // 4 % 2, rows, :] = two[s]
    first_hop = []
    for half, axis in enumerate("zx"):
        for i in range(1, 4):
            dev, q = peer_on(at, axis, i)
            cp = rcopy(
                r.gb.at[half, pl.ds(q * 8, 8)],
                r.gb1.at[half, i - 1],
                r.b1s.at[half, i - 1],
                r.b1r.at[half, i - 1],
                dev,
            )
            cp.start()
            first_hop.append(cp)
    for g in FIRST:
        sums.rs_end(g, 0)
        sums.rs_start(g, 1)
    attended = r.acc[0]
    gated = (r.gsig[...] * attended).astype(BF)
    r.gheads[:, 1152:] = (r.ggat[...] * attended * r.gsig[...] * (1.0 - r.gsig[...])).astype(BF)
    grad_q = (r.acc[1] * SCALE).astype(BF)
    r.gheads[:, :384] = grad_q
    r.gheads[:, 384:768] = (r.acc[2] * SCALE).astype(BF)
    r.gheads[:, 768:1152] = r.acc[3].astype(BF)
    for j in range(3):
        r.small_w[9 + j : 10 + j] = jnp.sum(
            grad_q[:, j * 128 : (j + 1) * 128].astype(F32), 0, keepdims=True
        )
    for b in blocks:
        branch_out(0, b, dot(gated, r.wout[:, b]))
    r.mixs[...] = r.mixf[...].astype(BF)
    mix_copy = rcopy(r.mixs, r.mixr, r.hs.at[1], r.hr.at[1], head_dev(at))
    mix_copy.start()
    r.flipped[:384] = flip(gated)
    for i, b in enumerate(blocks):
        put(r.tiles[2], T_OUT + i * 48, dot(r.flipped[:384], r.gao[:, b]))
    r.flipped[...] = flip(r.ain[...])
    for i in range(6):
        put(r.tiles[2], T_QKVG + i * 96, dot(r.flipped[...], r.gheads[:, i * 256 : (i + 1) * 256]))
    r.tiles[2][T_WPAD:] = jnp.zeros((TILES[2] - T_WPAD, 16, 128), BF)
    sums.core_start(2)
    for g in FIRST:
        sums.rs_end(g, 1)
        sums.rs_start(g, 2)
    for b in blocks:
        total = dot_t(r.gheads[:, :384], r.wq[0, b, :])
        for k in range(1, 4):
            total = total + dot_t(r.gheads[:, k * 384 : (k + 1) * 384], r.wq[k, b, :])
        branch_in(0, b, total)
    r.acts[...] = r.actf[...].astype(BF)
    act_copy = rcopy(r.acts, r.actr, r.hs.at[2], r.hr.at[2], head_dev(at))
    act_copy.start()
    sums.core_end(2)
    sums.rs_start(4, 0)
    sums.rs_start(5, 0)
    for cp in first_hop:
        cp.wait()
    second_hop = []
    for half in range(2):
        own = pl.ds(at["zx"[half]] * 8, 8)
        total = r.gb[half, own].astype(F32)
        for i in range(3):
            total = total + r.gb1[half, i].astype(F32)
        r.gb[half, own] = total.astype(BF)
        for i in range(1, 8):
            if half == 0:
                lo, x = (at["l"] + i // 4) % 2, (at["x"] + i % 4) % 4
                dev, q = samp_dev(at, at["z"] * 8 + lo * 4 + x), lo * 4 + x
            else:
                z, lo = (at["z"] + i // 2) % 4, (at["l"] + i % 2) % 2
                dev, q = samp_dev(at, z * 8 + lo * 4 + at["x"]), z * 2 + lo
            cp = rcopy(
                r.gb.at[half, at["zx"[half]] * 8 + q],
                r.gb2.at[half, i - 1],
                r.b2s.at[half, i - 1],
                r.b2r.at[half, i - 1],
                dev,
            )
            cp.start()
            second_hop.append(cp)
    conditioned(0, r.tiles[3])
    conditioning_back(0)
    grad_single = norm_back(r.gsh[...], r.shat[...], r.sinv[:, :1]) + r.zterm[...]
    put(r.tiles[4], 0, grad_single)
    r.tiles[4][48:] = jnp.zeros((TILES[4] - 48, 16, 128), BF)
    r.tiles[3][T_SMALL:T_APAD] = r.small_a[...].astype(BF).reshape(2, 16, 128)
    r.tiles[3][T_APAD:] = jnp.zeros((TILES[3] - T_APAD, 16, 128), BF)
    sums.core_start(3)
    sums.rs_start(8, 0)
    for g in FIRST:
        sums.rs_end(g, 2)
        sums.ag_start(g, 2)
    sums.core_end(3)
    sums.rs_start(6, 0)
    sums.rs_start(7, 0)
    for cp in second_hop:
        cp.wait()
    places = (at["z"] * 8 + at["l"] * 4 + at["x"], at["x"] * 8 + at["z"] * 2 + at["l"])
    for half in range(2):
        total = r.gb[half, places[half]].astype(F32)
        for i in range(7):
            total = total + r.gb2[half, i].astype(F32)
        r.gball[hd, half * 32 : half * 32 + 32] = total.astype(BF)
    rows_copy = rcopy(r.gball.at[hd], r.gball.at[hd], r.hs.at[3], r.hr.at[3], head_dev(at))
    rows_copy.start()
    for g in FIRST:
        sums.ag_end(g, 2)
        sums.ag_start(g, 1)
    mix_copy.wait()

    def last_mix(i):
        rows = pl.ds(i * 16, 16)
        value = r.mixs[rows].astype(F32) + r.mixr[rows].astype(F32)
        r.hidden[rows] = (r.act[rows].astype(F32) + value).astype(BF)

    loop(16, last_mix)
    leave(r.hidden, "mixed_o")

    rows_copy.wait()
    r.rows[...] = r.gball[hd].astype(F32).reshape(8, 8, N)
    r.held[:16] = r.gball[...].astype(F32).reshape(16, 8, N)
    wt_all = (
        jnp.concatenate([r.wall[0].astype(F32)[:8], r.wall[1].astype(F32)[:8]], 0).astype(BF)
    )
    weight = jnp.zeros((8, 128), F32)
    total = jnp.zeros((1, 128), F32)
    for i in range(8):
        normed, inv = normalize(r.pair[i].astype(F32))
        weight = weight + dot(r.rows[:, i, :].astype(BF), (normed * pgain).astype(BF))
        grad_low = dot_l(r.held[:16, i, :].astype(BF), wt_all)
        total = total + jnp.sum(grad_low * normed, 0, keepdims=True)
        r.gpair[i] = norm_back(grad_low * pgain, normed, inv)
    leave(r.gpair, "pair_o")
    r.small_w[:8] = weight
    r.small_w[8:9] = total

    def small_start(k):
        axis = "czxl"[k]
        mine = at[axis]
        r.slot[k, mine] = r.small_w[...]
        cps = []
        for i in range(1, SIZE.get(axis, 2)):
            dev = core_dev(at) if axis == "c" else peer_on(at, axis, i)[0]
            cp = rcopy(
                r.slot.at[k, mine], r.slot.at[k, mine], r.ss.at[k, i - 1], r.sr.at[k, i - 1], dev
            )
            cp.start()
            cps.append(cp)
        return cps

    def small_end(k, cps):
        for cp in cps:
            cp.wait()
        total = r.slot[k, 0]
        for i in range(1, SIZE.get("czxl"[k], 2)):
            total = total + r.slot[k, i]
        r.small_w[...] = total

    tiny = small_start(0)
    for g in SECOND:
        sums.rs_end(g, 0)
        sums.rs_start(g, 1)
    small_end(0, tiny)
    tiny = small_start(1)
    for g in FIRST:
        sums.ag_end(g, 1)
        sums.ag_start(g, 0)
    act_copy.wait()

    def last_act(i):
        rows = pl.ds(i * 16, 16)
        grad = r.acts[rows].astype(F32) + r.actr[rows].astype(F32)
        normed, inv = normalize(r.act[rows].astype(F32))
        r.mixf[rows] = r.cot[rows].astype(F32) + norm_back(grad, normed, inv)

    loop(16, last_act)
    leave(r.mixf, "act_o")
    for g in SECOND:
        sums.rs_end(g, 1)
        sums.rs_start(g, 2)
    small_end(1, tiny)
    tiny = small_start(2)
    for g in FIRST:
        sums.ag_end(g, 0)
        sums.share_start(g)
    for g in SECOND:
        sums.rs_end(g, 2)
        sums.ag_start(g, 2)
    small_end(2, tiny)
    tiny = small_start(3)
    for g in SECOND:
        sums.ag_end(g, 2)
        sums.ag_start(g, 1)
    for g in FIRST:
        sums.share_end(g)
    for b in (0, 1):
        leave(r.sums[b], "sum%d" % b)
    small_end(3, tiny)
    leave(r.small_w, "small_o")
    for g in SECOND:
        sums.ag_end(g, 1)
        sums.ag_start(g, 0)
    for g in SECOND:
        sums.ag_end(g, 0)
        sums.share_start(g)
    leave(r.sums[4], "sum4")
    for g in SECOND:
        sums.share_end(g)
    for b in (2, 3):
        leave(r.sums[b], "sum%d" % b)
    for cp in copies:
        cp.wait()


def whole(shape, dtype):
    return jax.ShapeDtypeStruct(shape, dtype)


def mega(counts, *args):
    return pl.pallas_call(
        mega_kernel,
        out_shape=tuple(whole(shape, dtype) for _, shape, dtype in OUTPUTS),
        in_specs=[pl.BlockSpec(memory_space=pltpu.SMEM)]
        + [pl.BlockSpec(memory_space=pl.ANY)] * len(INPUTS),
        out_specs=[pl.BlockSpec(memory_space=pl.ANY)] * len(OUTPUTS),
        scratch_shapes=[pltpu.VMEM(shape, BF) for _, shape in INPUTS]
        + [pltpu.VMEM(shape, dtype) for _, shape, dtype in SCRATCH]
        + [pltpu.VMEM((t, 16, 128), BF) for t in TILES]
        + [pltpu.VMEM((t, 16, 128), BF) for t in TILES]
        + [pltpu.VMEM(shape, BF) for _, shape in recv_shapes()]
        + [pltpu.SemaphoreType.DMA(shape) for _, shape in SEMS],
        compiler_params=pltpu.CompilerParams(
            collective_id=0, has_side_effects=True, vmem_limit_bytes=63 * 2**20
        ),
        name="block",
    )(counts, *args)


FINAL = (
    ("qkvg", (D, 4, 384)),
    ("win", (D, 2, D)),
    ("hid", (D, D)),
    ("ada", (2, 384, 2 * D)),
    ("zero", (2, 384, D)),
    ("wout", (384, D)),
    ("single", (N, 384)),
    ("adab", (2, D)),
    ("zerob", (2, D)),
    ("gain", (2, 384)),
    ("wt", (8, 128)),
    ("qb", (384,)),
    ("pgain", (128,)),
)


def finish_kernel(*refs):
    refs = list(refs)

    def take(count):
        got = refs[:count]
        del refs[:count]
        return got

    ins = take(9)
    outs = take(3 + len(FINAL))
    held = take(9)
    f = Refs()
    for (name, _), ref in zip(FINAL, take(len(FINAL))):
        setattr(f, name, ref)
    in_sem, out_sem = take(2)
    loads = []
    for i in range(9):
        cp = pltpu.make_async_copy(ins[i], held[i], in_sem.at[i])
        cp.start()
        loads.append(cp)
    copies = []

    def leave(name):
        i = [k for k, _ in FINAL].index(name)
        cp = pltpu.make_async_copy(getattr(f, name), outs[3 + i], out_sem.at[3 + i])
        cp.start()
        copies.append(cp)

    def get(b, start, rows):
        return held[b][pl.ds(start, rows // 16)].astype(F32).reshape(rows, 128)

    cols = [slice(j * 128, (j + 1) * 128) for j in range(12)]
    loads[0].wait()
    for k in range(2):
        for j in range(6):
            f.win[:, k, cols[j]] = get(0, T_IN + (k * 6 + j) * 48, 768)
    leave("win")
    for i in range(3):
        loads[6 + i].wait()
        cp = pltpu.make_async_copy(held[6 + i], outs[i], out_sem.at[i])
        cp.start()
        copies.append(cp)
    loads[2].wait()
    for j in range(5):
        f.hid[:, cols[j]] = get(0, T_HID + j * 48, 768)
    f.hid[:256, cols[5]] = get(0, T_HID + 240, 256)
    f.hid[256:, cols[5]] = get(2, T_HID2, 512)
    leave("hid")
    for k in range(4):
        for j in range(3):
            f.qkvg[:, k, cols[j]] = get(2, T_QKVG + (k * 3 + j) * 48, 768)
    leave("qkvg")
    for j in range(6):
        f.wout[:, cols[j]] = get(2, T_OUT + j * 24, 384)
    leave("wout")
    loads[1].wait()
    loads[3].wait()
    for w in range(2):
        for j in range(12):
            f.ada[w, :, cols[j]] = get(3 - 2 * w, T_ADA[w] + j * 24, 384)
    leave("ada")
    for w in range(2):
        for j in range(6):
            if w == 1 and j >= 4:
                f.zero[w, :, cols[j]] = get(3, T_ZERO2 + (j - 4) * 24, 384)
            else:
                f.zero[w, :, cols[j]] = get(3 - 2 * w, T_ZERO[w] + j * 24, 384)
    leave("zero")
    loads[4].wait()
    for j in range(3):
        f.single[:, cols[j]] = get(4, j * 16, 256)
    leave("single")
    small = held[3][T_SMALL:T_APAD].astype(F32).reshape(32, 128)
    for w in range(2):
        for j in range(6):
            f.adab[w : w + 1, cols[j]] = small[6 * w + j : 6 * w + j + 1]
            f.zerob[w : w + 1, cols[j]] = small[12 + 6 * w + j : 13 + 6 * w + j]
        for j in range(3):
            f.gain[w : w + 1, cols[j]] = small[24 + 3 * w + j : 25 + 3 * w + j]
    loads[5].wait()
    f.wt[...] = held[5][:8]
    f.pgain[...] = held[5][8]
    for j in range(3):
        f.qb[cols[j]] = held[5][9 + j]
    for name in ("adab", "zerob", "gain", "wt", "pgain", "qb"):
        leave(name)
    for cp in copies:
        cp.wait()


def finish(*args):
    shapes = [whole((N, D), BF), whole((N, D), F32), whole((8, N, 128), F32)]
    shapes += [whole(shape, F32) for _, shape in FINAL]
    return pl.pallas_call(
        finish_kernel,
        out_shape=tuple(shapes),
        in_specs=[pl.BlockSpec(memory_space=pl.ANY)] * len(args),
        out_specs=[pl.BlockSpec(memory_space=pl.ANY)] * len(shapes),
        scratch_shapes=[pltpu.VMEM(a.shape, a.dtype) for a in args]
        + [pltpu.VMEM(shape, F32) for _, shape in FINAL]
        + [pltpu.SemaphoreType.DMA((9,)), pltpu.SemaphoreType.DMA((len(shapes),))],
        compiler_params=pltpu.CompilerParams(vmem_limit_bytes=60 * 2**20),
        name="finish",
    )(*args)


def local(
    activations,
    conditioning,
    pair,
    counts,
    ada_weight,
    ada_bias,
    cond_gain,
    zero_weight,
    zero_bias,
    qkvg_weight,
    q_bias,
    out_weight,
    in_weight,
    hid_weight,
    pair_gain,
    bias_weight,
    cotangent,
):
    results = mega(
        counts,
        pair[0],
        pair_gain,
        bias_weight.T,
        conditioning[0],
        cond_gain,
        ada_weight,
        ada_bias,
        zero_weight,
        zero_bias,
        activations[0, 0],
        cotangent[0, 0],
        in_weight.transpose(1, 0, 2),
        hid_weight,
        qkvg_weight.transpose(1, 0, 2),
        q_bias,
        out_weight,
    )
    outs = finish(*results)
    mixed, act, grad_pair = outs[:3]
    o = dict(zip([name for name, _ in FINAL], outs[3:]))
    return (
        mixed[None, None],
        act[None, None],
        o["single"][None],
        grad_pair[None],
        o["ada"],
        o["adab"],
        o["gain"],
        o["zero"],
        o["zerob"],
        o["qkvg"],
        o["qb"],
        o["wout"],
        o["win"],
        o["hid"],
        o["pgain"],
        o["wt"].T,
    )


def solution(mesh):
    placed = (
        P("cplx", "samp", None, None),
        P("cplx", None, None),
        P("cplx", "samp", None, None),
        P("cplx"),
        P(),
        P(),
        P(),
        P(),
        P(),
        P(None, None, "head"),
        P("head"),
        P("head", None),
        P(None, None, "head"),
        P("head", None),
        P(),
        P(None, "head"),
        P("cplx", "samp", None, None),
    )
    return jax.shard_map(
        local,
        mesh=mesh,
        in_specs=placed,
        out_specs=(
            P("cplx", "samp", None, None),
            P("cplx", "samp", None, None),
            P("cplx", None, None),
            P("cplx", "samp", None, None),
            P(),
            P(),
            P(),
            P(),
            P(),
            P(None, None, "head"),
            P("head"),
            P("head", None),
            P(None, None, "head"),
            P("head", None),
            P(),
            P(None, "head"),
        ),
        check_vma=False,
    )
```

time: 1410 us -> 145 us (0.10)
  waiting for transfers between devices: 968 us -> 0 us
  blocking collectives: 283 us -> 0 us
  Pallas kernels: 0 us -> 138 us
  matrix products: 64.5 us -> 0 us
  local copies, waits for them, and re-layouts: 46.2 us -> 5.23 us
  other arithmetic: 24 us -> 0 us
    psum x3 -> x0, waiting for transfers between devices: 731 us -> none  [the longest x1 649 us: local(): lax.psum((grad_ada_weight, grad_ada_bias, grad_cond_gain, grad_zero_weigh...]
    psum x1 -> x0, blocking collectives: 283 us -> none  [local(): lax.psum((grad_ada_weight, grad_ada_bias, grad_cond_gain, grad_zero_weigh...]
    pallas_call x0 -> x2, Pallas kernels: none -> 138 us  [the longest x1 125 us: mega(): pl.pallas_call(mega_kernel, out_shape=tuple((whole(shape, dtype) for _, s...]
    reduce_scatter x1 -> x0, waiting for transfers between devices: 133 us -> none  [local(): lax.psum_scatter(grad_bias_part.astype(jnp.bfloat16), 'samp', scatter_dim...]
    all_gather x1 -> x0, waiting for transfers between devices: 104 us -> none  [local(): pair_bias = lax.all_gather(bias_part, 'samp', axis=1, tiled=True)]
    dot_general x27 -> x0, matrix products: 64.5 us -> none  [the longest x1 5.67 us: local(): jnp.einsum('wnc,wnd->wcd', scaled, grad_ada_pre, precision=HIGH)]
    unnamed x176 -> x4, local copies, waits for them, and re-layouts: 31.2 us -> 5.23 us
  transfers between devices with their start and end apart: 5 -> 0, of which waited for: 4 -> 0; matrix products, arithmetic and copies ran while one was open for 5% -> 0% of each run, Pallas kernels for 0% -> 0%
where the time goes in v1:
time: 145 us; the launch traced here: 144 us
  Pallas kernels  138 us (95%)
  local copies, waits for them, and re-layouts  5.23 us (4%)
  between operations  1.49 us (1%)
    pallas_call x1, Pallas kernels, mega(): pl.pallas_call(mega_kernel, out_shape=tuple((whole(shape, dtype) for _, s...  125 us
    pallas_call x1, Pallas kernels, finish(): pl.pallas_call(finish_kernel, out_shape=tuple(shapes), in_specs=[pl.Block...  12.3 us
    unnamed x4, local copies, waits for them, and re-layouts  5.23 us

profile of v1, /device:TPU:1, one launch (start us, length us, event | category | flops | bytes accessed | tf_op | source)
XLA Modules:
  0.0 144.4 jit_solution(17820431300980060303)
XLA Ops:
  1.3 0.0 copy-start
  1.3 3.5 %copy.37 = bf16[768,4,384]{2,0,1:T(8,128)(2,1)} copy(bf16[768,4,384]{2,1,0:T(4,128)(2,1)} %param.26) | data formatting | bytes 4718592 | tf_op args[9]
  4.8 0.0 copy-done
  4.8 1.7 %copy.38 = bf16[768,2,768]{2,0,1:T(8,128)(2,1)} copy(bf16[768,2,768]{2,1,0:T(2,128)(2,1)S(1)} %copy-done) | data formatting | bytes 4718592 | tf_op args[12]
  6.5 125.4 %block.1 = (bf16[832,16,128]{2,1,0:T(8,128)(2,1)}, bf16[384,16,128]{2,1,0:T(8,128)(2,1)}, bf16[768,16,128]{2,1,0:T(8,128)(2,1)}, bf16[512,16,128]{2,1,0:T(8,128)...) custom-call(s32[1]{0:T(128)S(6)} %copy.39.refs_0_, ...), custom_call_target="tpu_custom_call" | custom-call | tf_op jit(solution)/shard_map/block/pallas_call | solution.py:849
  131.9 12.3 %finish.1 = (bf16[256,768]{1,0:T(8,128)(2,1)}, f32[256,768]{1,0:T(8,128)}, f32[8,256,128]{2,1,0:T(8,128)}, f32[768,4,384]{2,1,0:T(4,128)}, f32[768,2,768]{2,1,0:...) custom-call(bf16[832,16,128]{2,1,0:T(8,128)(2,1)} %get-tuple-element, ...), custom_call_target="tpu_custom_call" | custom-call | tf_op jit(solution)/shard_map/finish/pallas_call | solution.py:978
Async XLA Ops:
  1.3 3.5 %copy-start = (bf16[768,2,768]{2,1,0:T(2,128)(2,1)S(1)}, bf16[768,2,768]{2,1,0:T(2,128)(2,1)}, u32[]{:S(2)}) copy-start(bf16[768,2,768]{2,1,0:T(2,128)(2,1)} %param.29) | copy-start | bytes 7077892

commit v2 on v1

--- a/solution.py
+++ b/solution.py
@@ -35,18 +35,29 @@
 SIZE = {"z": 4, "x": 4, "y": 4, "l": 2}
 
 
-def peer_on(at, axis, step):
-    z, x, lo, hd = at["z"], at["x"], at["l"], at["h"]
-    q = (at[axis] + step) % SIZE[axis]
-    if axis == "z":
-        z = q
-    elif axis == "x":
-        x = q
-    elif axis == "l":
-        lo = q
-    else:
-        hd, lo = q // 2, q % 2
-    return {"cplx": at["c"], "samp": z * 8 + lo * 4 + x, "head": hd}, q
+def extent(axes):
+    size = 1
+    for a in axes:
+        size *= SIZE[a]
+    return size
+
+
+def index_on(at, axes):
+    index = 0
+    for a in axes:
+        index = index * SIZE[a] + at[a]
+    return index
+
+
+def peer_on(at, axes, step):
+    now = dict(at)
+    for a in reversed(axes):
+        now[a] = (at[a] + step % SIZE[a]) % SIZE[a]
+        step //= SIZE[a]
+    if "y" in axes:
+        now["h"], now["l"] = now["y"] // 2, now["y"] % 2
+    dev = {"cplx": at["c"], "samp": now["z"] * 8 + now["l"] * 4 + now["x"], "head": now["h"]}
+    return dev, index_on(now, axes)
 
 
 def signal(bar, dev):
@@ -136,18 +147,19 @@
 TILES = (832, 384, 768, 512, 64)
 HALF = (416, 192, 384, 256, 64)
 GROUPS = (
-    (0, 0, 192, "zxl"),
-    (0, 192, 224, "xzl"),
-    (1, 0, 128, "yzx"),
-    (1, 128, 64, "zyx"),
-    (2, 0, 192, "zxl"),
-    (2, 192, 192, "xzl"),
-    (3, 0, 192, "yxz"),
-    (3, 192, 64, "xyz"),
-    (4, 0, 64, "yzx"),
+    (0, 0, 192, ("z", "xl")),
+    (0, 192, 224, ("x", "zl")),
+    (1, 0, 128, ("y", "zx")),
+    (1, 128, 64, ("z", "yx")),
+    (2, 0, 192, ("z", "xl")),
+    (2, 192, 192, ("x", "zl")),
+    (3, 0, 128, ("y", "xz")),
+    (3, 128, 64, ("z", "yx")),
+    (3, 192, 64, ("x", "yz")),
+    (4, 0, 64, ("y", "zx")),
 )
 FIRST = (0, 1, 2, 3)
-SECOND = (4, 5, 6, 7, 8)
+SECOND = (4, 5, 6, 7, 8, 9)
 T_IN, T_HID = 0, 576
 T_ADA, T_ZERO = (0, 0), (288, 288)
 T_QKVG, T_OUT, T_HID2, T_WPAD = 0, 576, 720, 752
@@ -171,6 +183,10 @@
     ("qb", (384,)),
     ("wout", (384, 768)),
 )
+LOADS = (
+    ("pair", "pgain", "wt", "single", "gain", "adab", "zerob", "ada1", "zero1", "act", "cot")
+    + ("win", "hid", "ada0", "zero0", "wq", "qb", "wout")
+)
 N = 256
 SCRATCH = (
     ("rows", (8, 8, N), F32),
@@ -184,7 +200,7 @@
     ("s_t", (2, 384, N), BF),
     ("one_t", (384, N), BF),
     ("mg", (2, N, D), F32),
-    ("ms", (2, N, D), F32),
+    ("ms", (N, D), F32),
     ("zg", (2, N, D), F32),
     ("hat", (N, D), F32),
     ("ain", (N, D), BF),
@@ -221,26 +237,26 @@
     ("slot", (4, 4, 16, 128), F32),
 )
 SEMS = (
-    ("ld", (len(INPUTS),)),
-    ("bs", (NS,)),
-    ("br", (NS,)),
+    ("ld", (len(LOADS),)),
+    ("bs", (1,)),
+    ("br", (1,)),
     ("hs", (4,)),
     ("hr", (4,)),
-    ("cs", (5,)),
-    ("cr", (5,)),
-    ("rs", (len(GROUPS), 3, 3)),
-    ("rr", (len(GROUPS), 3, 3)),
-    ("gs", (len(GROUPS), 3, 3)),
-    ("gr", (len(GROUPS), 3, 3)),
-    ("fs", (len(GROUPS),)),
-    ("fr", (len(GROUPS),)),
-    ("b1s", (2, 3)),
-    ("b1r", (2, 3)),
-    ("b2s", (2, 7)),
-    ("b2r", (2, 7)),
-    ("ss", (4, 3)),
-    ("sr", (4, 3)),
-    ("out", (12,)),
+    ("cs", (4,)),
+    ("cr", (4,)),
+    ("rs", (len(GROUPS), 2)),
+    ("rr", (len(GROUPS), 2)),
+    ("gs", (len(GROUPS), 2)),
+    ("gr", (len(GROUPS), 2)),
+    ("fs", (4,)),
+    ("fr", (4,)),
+    ("b1s", (2,)),
+    ("b1r", (2,)),
+    ("b2s", (2,)),
+    ("b2r", (2,)),
+    ("out", (9,)),
+    ("ss", (4,)),
+    ("sr", (4,)),
 )
 OUTPUTS = tuple(("sum%d" % i, (t, 16, 128), BF) for i, t in enumerate(TILES)) + (
     ("small_o", (16, 128), F32),
@@ -258,9 +274,15 @@
     shapes = []
     for g, (_, _, tiles, axes) in enumerate(GROUPS):
         for s, axis in enumerate(axes):
-            tiles //= SIZE[axis]
-            shapes.append(((g, s), (SIZE[axis] - 1, tiles, 16, 128)))
+            tiles //= extent(axis)
+            shapes.append(((g, s), (extent(axis) - 1, tiles, 16, 128)))
     return shapes
+
+
+def arrived(like, send, recv, at):
+    cp = rcopy(like, like, send, recv, core_dev(at))
+    cp.wait_send()
+    cp.wait_recv()
 
 
 class Sums:
@@ -270,9 +292,7 @@
         self.shift = [core * HALF[b] if b < 4 else 0 for b in range(5)]
         self.base = [None] * len(GROUPS)
         self.part = [None] * len(GROUPS)
-        self.pending = [None] * len(GROUPS)
         self.pairs = {}
-        self.last = {}
 
     def core_start(self, buf):
         r, at, half = self.r, self.at, HALF[buf]
@@ -302,43 +322,39 @@
         r, at = self.r, self.at
         buf, start, tiles, axes = GROUPS[g]
         axis = axes[stage]
-        count = SIZE[axis]
+        count = extent(axis)
         for a in axes[:stage]:
-            tiles //= SIZE[a]
+            tiles //= extent(a)
         if stage == 0:
             self.base[g] = self.shift[buf] + start
         part = tiles // count
-        cps = []
         for i in range(1, count):
             dev, q = peer_on(at, axis, i)
-            cp = rcopy(
+            rcopy(
                 r.tiles[buf].at[pl.ds(self.base[g] + q * part, part)],
                 r.recv[g, stage].at[i - 1],
-                r.rs.at[g, stage, i - 1],
-                r.rr.at[g, stage, i - 1],
+                r.rs.at[g, stage],
+                r.rr.at[g, stage],
                 dev,
-            )
-            cp.start()
-            cps.append(cp)
-        self.pending[g] = cps
+            ).start()
         self.part[g] = part
 
     def rs_end(self, g, stage):
         r = self.r
         buf, _, _, axes = GROUPS[g]
         part = self.part[g]
-        for cp in self.pending[g]:
-            cp.wait()
-        here = self.base[g] + self.at[axes[stage]] * part
+        got = r.recv[g, stage]
+        arrived(got, r.rs.at[g, stage], r.rr.at[g, stage], self.at)
+        here = self.base[g] + index_on(self.at, axes[stage]) * part
         block = max(b for b in range(1, 17) if part % b == 0)
 
         def add(i):
             rows = pl.ds(i * block, block)
             mine = pl.ds(here + i * block, block)
             total = r.tiles[buf][mine].astype(F32)
-            for j in range(SIZE[axes[stage]] - 1):
+            for j in range(extent(axes[stage]) - 1):
                 total = total + r.recv[g, stage][j, rows].astype(F32)
-            to = r.sums if stage == 2 else r.tiles
+            to = r.sums if stage == 1 else r.tiles
             to[buf][mine] = total.astype(BF)
 
         loop(part // block, add)
@@ -348,41 +364,41 @@
         r = self.r
         buf, _, _, axes = GROUPS[g]
         rows = pl.ds(self.base[g], self.part[g])
-        cps = []
-        for i in range(1, SIZE[axes[stage]]):
+        for i in range(1, extent(axes[stage])):
             dev, _ = peer_on(self.at, axes[stage], i)
-            cp = rcopy(
+            rcopy(
                 r.sums[buf].at[rows],
                 r.sums[buf].at[rows],
-                r.gs.at[g, stage, i - 1],
-                r.gr.at[g, stage, i - 1],
+                r.gs.at[g, stage],
+                r.gr.at[g, stage],
                 dev,
-            )
-            cp.start()
-            cps.append(cp)
-        self.pending[g] = cps
+            ).start()
 
     def ag_end(self, g, stage):
-        axis = GROUPS[g][3][stage]
-        for cp in self.pending[g]:
-            cp.wait()
-        self.base[g] = self.base[g] - self.at[axis] * self.part[g]
-        self.part[g] = self.part[g] * SIZE[axis]
+        r = self.r
+        buf, _, _, axes = GROUPS[g]
+        axis = axes[stage]
+        count = (extent(axis) - 1) * self.part[g]
+        arrived(r.sums[buf].at[pl.ds(0, count)], r.gs.at[g, stage], r.gr.at[g, stage], self.at)
+        self.base[g] = self.base[g] - index_on(self.at, axis) * self.part[g]
+        self.part[g] = self.part[g] * extent(axis)
 
     def share_start(self, g):
         r = self.r
         buf, start, tiles, _ = GROUPS[g]
         if buf < 4:
             rows = pl.ds(self.shift[buf] + start, tiles)
-            cp = rcopy(
-                r.sums[buf].at[rows], r.sums[buf].at[rows], r.fs.at[g], r.fr.at[g], core_dev(self.at)
-            )
-            cp.start()
-            self.last[g] = cp
-
-    def share_end(self, g):
-        if g in self.last:
-            self.last[g].wait()
+            rcopy(
+                r.sums[buf].at[rows],
+                r.sums[buf].at[rows],
+                r.fs.at[buf],
+                r.fr.at[buf],
+                core_dev(self.at),
+            ).start()
+
+    def share_end(self, buf):
+        r = self.r
+        arrived(r.sums[buf].at[pl.ds(0, HALF[buf])], r.fs.at[buf], r.fr.at[buf], self.at)
 
 
 def mega_kernel(*refs):
@@ -413,8 +429,12 @@
     me, hd = at["s"], at["h"]
     blocks = [slice(i * 256, (i + 1) * 256) for i in range(3)]
     loads = {}
-    for i, (name, _) in enumerate(INPUTS):
-        cp = pltpu.make_async_copy(hbm[i], getattr(r, name), r.ld.at[i])
+    places = {name: i for i, (name, _) in enumerate(INPUTS)}
+    for k, name in enumerate(LOADS):
+        src, dst = hbm[places[name.rstrip("01")]], getattr(r, name.rstrip("01"))
+        if name[-1] in "01":
+            src, dst = src.at[int(name[-1])], dst.at[int(name[-1])]
+        cp = pltpu.make_async_copy(src, dst, r.ld.at[k])
         cp.start()
         loads[name] = cp
 
@@ -447,7 +467,7 @@
 
     def bias_copy(i):
         return rcopy(
-            r.part, r.bias.at[me], r.bs.at[i], r.br.at[i], samp_dev(at, (me + i) % NS)
+            r.part, r.bias.at[me], r.bs.at[0], r.br.at[0], samp_dev(at, (me + i) % NS)
         )
 
     loop(NS - 1, lambda i: bias_copy(i + 1).start())
@@ -471,32 +491,34 @@
             r.s_lo[w, rows] = (scaled - high.astype(F32)).astype(BF)
 
     loop(N // 32, cond)
-    for w in range(2):
-        r.s_t[w] = flip(r.s_hi[w])
-    r.one_t[...] = flip(r.single[...])
-    need("ada", "adab", "zero", "zerob")
-    adab = r.adab[...].astype(F32)
-    zerob = r.zerob[...].astype(F32)
-    for w in range(2):
+
+    def modulation(w):
+        adab = r.adab[...].astype(F32)
+        zerob = r.zerob[...].astype(F32)
         for b in blocks:
             later = slice(D + b.start, D + b.stop)
             pre_gate = dot(r.s_hi[w], r.ada[w, :, b]) + dot(r.s_lo[w], r.ada[w, :, b])
             r.mg[w, :, b] = sigmoid(pre_gate + adab[w : w + 1, b])
-            r.ms[w, :, b] = dot(r.s_hi[w], r.ada[w, :, later]) + dot(r.s_lo[w], r.ada[w, :, later])
+            r.ms[:, b] = dot(r.s_hi[w], r.ada[w, :, later]) + dot(r.s_lo[w], r.ada[w, :, later])
             r.zg[w, :, b] = sigmoid(dot(r.single[...], r.zero[w, :, b]) + zerob[w : w + 1, b])
+
+    def branch_start(w, x_ref, g_ref):
+        def some(i):
+            rows = pl.ds(i * 16, 16)
+            if w == 1:
+                normed, _ = normalize(r.act[rows].astype(F32))
+                r.hat[rows] = normed
+            else:
+                normed = r.hat[rows]
+            x_ref[rows] = (r.mg[w, rows] * normed + r.ms[rows]).astype(BF)
+            g_ref[rows] = (r.zg[w, rows] * r.cot[rows].astype(F32)).astype(BF)
+
+        loop(N // 16, some)
+
+    need("adab", "zerob", "ada1", "zero1")
+    modulation(1)
     need("act", "cot")
-
-    def norm_in(i):
-        rows = pl.ds(i * 16, 16)
-        normed, _ = normalize(r.act[rows].astype(F32))
-        r.hat[rows] = normed
-        r.ain[rows] = (r.mg[0, rows] * normed + r.ms[0, rows]).astype(BF)
-        r.tin[rows] = (r.mg[1, rows] * normed + r.ms[1, rows]).astype(BF)
-        g = r.cot[rows].astype(F32)
-        r.gao[rows] = (r.zg[0, rows] * g).astype(BF)
-        r.gto[rows] = (r.zg[1, rows] * g).astype(BF)
-
-    loop(N // 16, norm_in)
+    branch_start(1, r.tin, r.gto)
 
     def branch_out(w, b, part):
         gate = r.zg[w, :, b]
@@ -540,6 +562,9 @@
             r.gsh[:, b] = share if w == 1 else r.gsh[:, b] + share
             r.zterm[:, b] = through if w == 1 else r.zterm[:, b] + through
 
+    for w in range(2):
+        r.s_t[w] = flip(r.s_hi[w])
+    r.one_t[...] = flip(r.single[...])
     need("win", "hid")
     for b in blocks:
         gate_in = dot(r.tin[...], r.win[0, :, b])
@@ -575,7 +600,12 @@
     sums.core_end(0)
     sums.rs_start(0, 0)
     sums.rs_start(1, 0)
-    conditioning_back(1)
+    need("ada0", "zero0")
+    modulation(0)
+    branch_start(0, r.ain, r.gao)
+    sums.core_end(1)
+    sums.rs_start(2, 0)
+    sums.rs_start(3, 0)
 
     need("wq", "qb", "wout")
     r.qkv[0] = (dot(r.ain[...], r.wq[0]) + r.qb[...].astype(F32).reshape(1, 384)).astype(BF)
@@ -584,10 +614,8 @@
     r.gsig[...] = sigmoid(dot(r.ain[...], r.wq[3]))
     r.ggat[...] = dot_t(r.gao[...], r.wout[...])
     r.gatt[...] = (r.ggat[...] * r.gsig[...]).astype(BF)
-    sums.core_end(1)
-    sums.rs_start(2, 0)
-    sums.rs_start(3, 0)
-    loop(NS - 1, lambda i: bias_copy(i + 1).wait())
+    conditioning_back(1)
+    arrived(r.bias.at[pl.ds(0, NS - 1)], r.bs.at[0], r.br.at[0], at)
     wt_copy.wait()
     r.acc[...] = jnp.zeros(r.acc.shape, F32)
     lane = lax.broadcasted_iota(jnp.int32, (1, 256), 1)
@@ -628,22 +656,16 @@
             else:
                 for s in range(NS):
                     r.gb[1, s % 4 * 8 + s // 8 * 2 + s // 4 % 2, rows, :] = two[s]
-    first_hop = []
     for half, axis in enumerate("zx"):
         for i in range(1, 4):
             dev, q = peer_on(at, axis, i)
-            cp = rcopy(
+            rcopy(
                 r.gb.at[half, pl.ds(q * 8, 8)],
                 r.gb1.at[half, i - 1],
-                r.b1s.at[half, i - 1],
-                r.b1r.at[half, i - 1],
+                r.b1s.at[half],
+                r.b1r.at[half],
                 dev,
-            )
-            cp.start()
-            first_hop.append(cp)
-    for g in FIRST:
-        sums.rs_end(g, 0)
-        sums.rs_start(g, 1)
+            ).start()
     attended = r.acc[0]
     gated = (r.gsig[...] * attended).astype(BF)
     r.gheads[:, 1152:] = (r.ggat[...] * attended * r.gsig[...] * (1.0 - r.gsig[...])).astype(BF)
@@ -668,9 +690,6 @@
         put(r.tiles[2], T_QKVG + i * 96, dot(r.flipped[...], r.gheads[:, i * 256 : (i + 1) * 256]))
     r.tiles[2][T_WPAD:] = jnp.zeros((TILES[2] - T_WPAD, 16, 128), BF)
     sums.core_start(2)
-    for g in FIRST:
-        sums.rs_end(g, 1)
-        sums.rs_start(g, 2)
     for b in blocks:
         total = dot_t(r.gheads[:, :384], r.wq[0, b, :])
         for k in range(1, 4):
@@ -679,62 +698,52 @@
     r.acts[...] = r.actf[...].astype(BF)
     act_copy = rcopy(r.acts, r.actr, r.hs.at[2], r.hr.at[2], head_dev(at))
     act_copy.start()
+    conditioned(0, r.tiles[3])
+    conditioning_back(0)
+    r.tiles[3][T_SMALL:T_APAD] = r.small_a[...].astype(BF).reshape(2, 16, 128)
+    r.tiles[3][T_APAD:] = jnp.zeros((TILES[3] - T_APAD, 16, 128), BF)
+    sums.core_start(3)
+    for g in FIRST:
+        sums.rs_end(g, 0)
+        sums.rs_start(g, 1)
     sums.core_end(2)
     sums.rs_start(4, 0)
     sums.rs_start(5, 0)
-    for cp in first_hop:
-        cp.wait()
-    second_hop = []
     for half in range(2):
+        arrived(r.gb1.at[half], r.b1s.at[half], r.b1r.at[half], at)
         own = pl.ds(at["zx"[half]] * 8, 8)
         total = r.gb[half, own].astype(F32)
         for i in range(3):
             total = total + r.gb1[half, i].astype(F32)
         r.gb[half, own] = total.astype(BF)
         for i in range(1, 8):
-            if half == 0:
-                lo, x = (at["l"] + i // 4) % 2, (at["x"] + i % 4) % 4
-                dev, q = samp_dev(at, at["z"] * 8 + lo * 4 + x), lo * 4 + x
-            else:
-                z, lo = (at["z"] + i // 2) % 4, (at["l"] + i % 2) % 2
-                dev, q = samp_dev(at, z * 8 + lo * 4 + at["x"]), z * 2 + lo
-            cp = rcopy(
+            dev, q = peer_on(at, ("lx", "zl")[half], i)
+            rcopy(
                 r.gb.at[half, at["zx"[half]] * 8 + q],
                 r.gb2.at[half, i - 1],
-                r.b2s.at[half, i - 1],
-                r.b2r.at[half, i - 1],
+                r.b2s.at[half],
+                r.b2r.at[half],
                 dev,
-            )
-            cp.start()
-            second_hop.append(cp)
-    conditioned(0, r.tiles[3])
-    conditioning_back(0)
+            ).start()
+    sums.core_end(3)
+    for g in (6, 7, 8):
+        sums.rs_start(g, 0)
     grad_single = norm_back(r.gsh[...], r.shat[...], r.sinv[:, :1]) + r.zterm[...]
     put(r.tiles[4], 0, grad_single)
     r.tiles[4][48:] = jnp.zeros((TILES[4] - 48, 16, 128), BF)
-    r.tiles[3][T_SMALL:T_APAD] = r.small_a[...].astype(BF).reshape(2, 16, 128)
-    r.tiles[3][T_APAD:] = jnp.zeros((TILES[3] - T_APAD, 16, 128), BF)
-    sums.core_start(3)
-    sums.rs_start(8, 0)
+    sums.rs_start(9, 0)
     for g in FIRST:
-        sums.rs_end(g, 2)
-        sums.ag_start(g, 2)
-    sums.core_end(3)
-    sums.rs_start(6, 0)
-    sums.rs_start(7, 0)
-    for cp in second_hop:
-        cp.wait()
+        sums.rs_end(g, 1)
+        sums.ag_start(g, 1)
     places = (at["z"] * 8 + at["l"] * 4 + at["x"], at["x"] * 8 + at["z"] * 2 + at["l"])
     for half in range(2):
+        arrived(r.gb2.at[half], r.b2s.at[half], r.b2r.at[half], at)
         total = r.gb[half, places[half]].astype(F32)
         for i in range(7):
             total = total + r.gb2[half, i].astype(F32)
         r.gball[hd, half * 32 : half * 32 + 32] = total.astype(BF)
     rows_copy = rcopy(r.gball.at[hd], r.gball.at[hd], r.hs.at[3], r.hr.at[3], head_dev(at))
     rows_copy.start()
-    for g in FIRST:
-        sums.ag_end(g, 2)
-        sums.ag_start(g, 1)
     mix_copy.wait()
 
     def last_mix(i):
@@ -744,6 +753,9 @@
 
     loop(16, last_mix)
     leave(r.hidden, "mixed_o")
+    for g in FIRST:
+        sums.ag_end(g, 1)
+        sums.ag_start(g, 0)
 
     rows_copy.wait()
     r.rows[...] = r.gball[hd].astype(F32).reshape(8, 8, N)
@@ -767,33 +779,23 @@
         axis = "czxl"[k]
         mine = at[axis]
         r.slot[k, mine] = r.small_w[...]
-        cps = []
         for i in range(1, SIZE.get(axis, 2)):
             dev = core_dev(at) if axis == "c" else peer_on(at, axis, i)[0]
-            cp = rcopy(
-                r.slot.at[k, mine], r.slot.at[k, mine], r.ss.at[k, i - 1], r.sr.at[k, i - 1], dev
-            )
-            cp.start()
-            cps.append(cp)
-        return cps
-
-    def small_end(k, cps):
-        for cp in cps:
-            cp.wait()
+            rcopy(r.slot.at[k, mine], r.slot.at[k, mine], r.ss.at[k], r.sr.at[k], dev).start()
+
+    def small_end(k):
+        arrived(r.slot.at[k, pl.ds(0, SIZE.get("czxl"[k], 2) - 1)], r.ss.at[k], r.sr.at[k], at)
         total = r.slot[k, 0]
         for i in range(1, SIZE.get("czxl"[k], 2)):
             total = total + r.slot[k, i]
         r.small_w[...] = total
 
-    tiny = small_start(0)
+    small_start(0)
     for g in SECOND:
         sums.rs_end(g, 0)
         sums.rs_start(g, 1)
-    small_end(0, tiny)
-    tiny = small_start(1)
-    for g in FIRST:
-        sums.ag_end(g, 1)
-        sums.ag_start(g, 0)
+    small_end(0)
+    small_start(1)
     act_copy.wait()
 
     def last_act(i):
@@ -804,38 +806,30 @@
 
     loop(16, last_act)
     leave(r.mixf, "act_o")
+    small_end(1)
+    small_start(2)
     for g in SECOND:
         sums.rs_end(g, 1)
-        sums.rs_start(g, 2)
-    small_end(1, tiny)
-    tiny = small_start(2)
+        sums.ag_start(g, 1)
+    small_end(2)
+    small_start(3)
     for g in FIRST:
         sums.ag_end(g, 0)
         sums.share_start(g)
     for g in SECOND:
-        sums.rs_end(g, 2)
-        sums.ag_start(g, 2)
-    small_end(2, tiny)
-    tiny = small_start(3)
-    for g in SECOND:
-        sums.ag_end(g, 2)
-        sums.ag_start(g, 1)
-    for g in FIRST:
-        sums.share_end(g)
-    for b in (0, 1):
-        leave(r.sums[b], "sum%d" % b)
-    small_end(3, tiny)
-    leave(r.small_w, "small_o")
-    for g in SECOND:
         sums.ag_end(g, 1)
         sums.ag_start(g, 0)
+    small_end(3)
+    leave(r.small_w, "small_o")
+    for b in (0, 1):
+        sums.share_end(b)
+        leave(r.sums[b], "sum%d" % b)
     for g in SECOND:
         sums.ag_end(g, 0)
         sums.share_start(g)
     leave(r.sums[4], "sum4")
-    for g in SECOND:
-        sums.share_end(g)
     for b in (2, 3):
+        sums.share_end(b)
         leave(r.sums[b], "sum%d" % b)
     for cp in copies:
         cp.wait()
@@ -983,7 +977,7 @@
         scratch_shapes=[pltpu.VMEM(a.shape, a.dtype) for a in args]
         + [pltpu.VMEM(shape, F32) for _, shape in FINAL]
         + [pltpu.SemaphoreType.DMA((9,)), pltpu.SemaphoreType.DMA((len(shapes),))],
-        compiler_params=pltpu.CompilerParams(vmem_limit_bytes=60 * 2**20),
+        compiler_params=pltpu.CompilerParams(vmem_limit_bytes=48 * 2**20),
         name="finish",
     )(*args)
 

time: 145 us -> 142 us (0.979)
  Pallas kernels: 138 us -> 127 us
  local copies, waits for them, and re-layouts: 5.23 us -> 13.2 us
    pallas_call x1, Pallas kernels: 125 us -> 114 us  [mega(): pl.pallas_call(mega_kernel, out_shape=tuple((whole(shape, dtype) for _, s...]
    unnamed x4 -> x18, local copies, waits for them, and re-layouts: 5.23 us -> 13.2 us
where the time goes in v2:
time: 142 us; the launch traced here: 141 us
  Pallas kernels  127 us (89%)
  local copies, waits for them, and re-layouts  13.2 us (9%)
  between operations  1.51 us (1%)
    pallas_call x1, Pallas kernels, mega(): pl.pallas_call(mega_kernel, out_shape=tuple((whole(shape, dtype) for _, s...  114 us
    unnamed x18, local copies, waits for them, and re-layouts  13.2 us
    pallas_call x1, Pallas kernels, finish(): pl.pallas_call(finish_kernel, out_shape=tuple(shapes), in_specs=[pl.Block...  12.3 us

profile of v2, /device:TPU:1, one launch (start us, length us, event | category | flops | bytes accessed | tf_op | source)
XLA Modules:
  0.0 141.2 jit_solution(801943379602900210)
XLA Ops:
  1.3 0.0 copy-start.7
  1.3 3.5 %copy.37 = bf16[768,4,384]{2,0,1:T(8,128)(2,1)} copy(bf16[768,4,384]{2,1,0:T(4,128)(2,1)} %param.26) | data formatting | bytes 4718592 | tf_op args[9]
  4.8 0.0 copy-done.7
  4.8 1.7 %copy.38 = bf16[768,2,768]{2,0,1:T(8,128)(2,1)} copy(bf16[768,2,768]{2,1,0:T(2,128)(2,1)S(1)} %copy-done.7) | data formatting | bytes 4718592 | tf_op args[12]
  6.5 114.2 %block.1 = (bf16[832,16,128]{2,1,0:T(8,128)(2,1)}, bf16[384,16,128]{2,1,0:T(8,128)(2,1)}, bf16[768,16,128]{2,1,0:T(8,128)(2,1)}, bf16[512,16,128]{2,1,0:T(8,128)...) custom-call(s32[1]{0:T(128)S(6)} %copy.39.refs_0_, ...), custom_call_target="tpu_custom_call" | custom-call | tf_op jit(solution)/shard_map/block/pallas_call | solution.py:843
  120.7 0.0 copy-start
  120.7 1.6 %copy-done = bf16[512,16,128]{2,1,0:T(8,128)(2,1)S(1)} copy-done((bf16[512,16,128]{2,1,0:T(8,128)(2,1)S(1)}, bf16[512,16,128]{2,1,0:T(8,128)(2,1)}, u32[]{:S(2)}) %copy-start) | copy-done | bytes 2097176
  122.3 0.0 copy-start.1
  122.3 1.4 copy-done.1
  123.7 0.0 copy-start.2
  123.7 1.2 copy-done.2
  125.0 0.0 copy-start.3
  125.0 1.1 copy-done.3
  126.1 0.0 copy-start.4
  126.1 1.0 copy-done.4
  127.1 0.0 copy-start.5
  127.1 0.9 copy-done.5
  128.0 0.0 copy-start.6
  128.0 0.7 copy-done.6
  128.7 12.3 %finish.1 = (bf16[256,768]{1,0:T(8,128)(2,1)}, f32[256,768]{1,0:T(8,128)}, f32[8,256,128]{2,1,0:T(8,128)}, f32[768,4,384]{2,1,0:T(4,128)}, f32[768,2,768]{2,1,0:...) custom-call(bf16[832,16,128]{2,1,0:T(8,128)(2,1)} %get-tuple-element, ...), custom_call_target="tpu_custom_call" | custom-call | tf_op jit(solution)/shard_map/finish/pallas_call | solution.py:972
Async XLA Ops:
  1.3 3.5 %copy-start.7 = (bf16[768,2,768]{2,1,0:T(2,128)(2,1)S(1)}, bf16[768,2,768]{2,1,0:T(2,128)(2,1)}, u32[]{:S(2)}) copy-start(bf16[768,2,768]{2,1,0:T(2,128)(2,1)} %param.29) | copy-start | bytes 7077892
  120.7 1.6 %copy-start = (bf16[512,16,128]{2,1,0:T(8,128)(2,1)S(1)}, bf16[512,16,128]{2,1,0:T(8,128)(2,1)}, u32[]{:S(2)}) copy-start(bf16[512,16,128]{2,1,0:T(8,128)(2,1)} %get-tuple-element.44.refs_3_) | copy-start | bytes 6291460
  122.3 1.4 copy-start.1
  123.7 1.2 copy-start.2
  125.0 1.1 copy-start.3
  126.1 1.0 copy-start.4
  127.1 0.9 copy-start.5
  128.0 0.7 copy-start.6

commit v3 on v2

--- a/solution.py
+++ b/solution.py
@@ -144,25 +144,26 @@
         )
 
 
-TILES = (832, 384, 768, 512, 64)
-HALF = (416, 192, 384, 256, 64)
+TILES = (384, 448, 384, 768, 512, 64)
+HALF = (192, 224, 192, 384, 256, 64)
 GROUPS = (
-    (0, 0, 192, ("z", "xl")),
-    (0, 192, 224, ("x", "zl")),
-    (1, 0, 128, ("y", "zx")),
-    (1, 128, 64, ("z", "yx")),
-    (2, 0, 192, ("z", "xl")),
-    (2, 192, 192, ("x", "zl")),
-    (3, 0, 128, ("y", "xz")),
-    (3, 128, 64, ("z", "yx")),
-    (3, 192, 64, ("x", "yz")),
-    (4, 0, 64, ("y", "zx")),
+    (0, 0, 192, "z", "xl"),
+    (1, 0, 224, "x", "zl"),
+    (2, 0, 64, "y", "zx"),
+    (2, 64, 64, "z", "yx"),
+    (2, 128, 64, "x", "yz"),
+    (3, 0, 192, "z", "xl"),
+    (3, 192, 192, "x", "zl"),
+    (4, 0, 128, "y", "xz"),
+    (4, 128, 64, "z", "yx"),
+    (4, 192, 64, "x", "yz"),
+    (5, 0, 64, "y", "zx"),
 )
-FIRST = (0, 1, 2, 3)
-SECOND = (4, 5, 6, 7, 8, 9)
-T_IN, T_HID = 0, 576
+FIRST = (0, 1, 2, 3, 4)
+SECOND = (5, 6, 7, 8, 9, 10)
+T_HID, T_IN0, T_IN = 0, 288, 0
 T_ADA, T_ZERO = (0, 0), (288, 288)
-T_QKVG, T_OUT, T_HID2, T_WPAD = 0, 576, 720, 752
+T_QKVG, T_OUT, T_IN2, T_WPAD = 0, 576, 720, 752
 T_ZERO2, T_SMALL, T_APAD = 432, 480, 482
 
 INPUTS = (
@@ -242,19 +243,17 @@
     ("br", (1,)),
     ("hs", (4,)),
     ("hr", (4,)),
-    ("cs", (4,)),
-    ("cr", (4,)),
-    ("rs", (len(GROUPS), 2)),
-    ("rr", (len(GROUPS), 2)),
-    ("gs", (len(GROUPS), 2)),
-    ("gr", (len(GROUPS), 2)),
-    ("fs", (4,)),
-    ("fr", (4,)),
+    ("cs", (5,)),
+    ("cr", (5,)),
+    ("rs", (len(GROUPS), 6)),
+    ("rr", (len(GROUPS), 6)),
+    ("fs", (5,)),
+    ("fr", (5,)),
     ("b1s", (2,)),
     ("b1r", (2,)),
     ("b2s", (2,)),
     ("b2r", (2,)),
-    ("out", (9,)),
+    ("out", (12,)),
     ("ss", (4,)),
     ("sr", (4,)),
 )
@@ -272,10 +271,12 @@
 
 def recv_shapes():
     shapes = []
-    for g, (_, _, tiles, axes) in enumerate(GROUPS):
-        for s, axis in enumerate(axes):
-            tiles //= extent(axis)
-            shapes.append(((g, s), (extent(axis) - 1, tiles, 16, 128)))
+    for g, (_, _, tiles, _, plane) in enumerate(GROUPS):
+        part = tiles // 4
+        small = part // extent(plane)
+        shapes.append(((g, "opp"), (2, part // 2, 16, 128)))
+        shapes.append(((g, "near"), (2, part, 16, 128)))
+        shapes.append(((g, "plane"), (extent(plane) - 1, small, 16, 128)))
     return shapes
 
 
@@ -288,113 +289,131 @@
 class Sums:
     def __init__(self, r, at):
         self.r, self.at = r, at
-        core = at["c"]
-        self.shift = [core * HALF[b] if b < 4 else 0 for b in range(5)]
-        self.base = [None] * len(GROUPS)
-        self.part = [None] * len(GROUPS)
+        self.shift = [at["c"] * HALF[b] if b < 5 else 0 for b in range(6)]
         self.pairs = {}
 
     def core_start(self, buf):
         r, at, half = self.r, self.at, HALF[buf]
+        other = pl.ds((1 - at["c"]) * half, half)
         cp = rcopy(
-            r.tiles[buf].at[pl.ds((1 - at["c"]) * half, half)],
-            r.sums[buf].at[pl.ds((1 - at["c"]) * half, half)],
-            r.cs.at[buf],
-            r.cr.at[buf],
-            core_dev(at),
+            r.tiles[buf].at[other], r.sums[buf].at[other], r.cs.at[buf], r.cr.at[buf], core_dev(at)
         )
         cp.start()
         self.pairs[buf] = cp
 
     def core_end(self, buf):
-        r, half, start = self.r, HALF[buf], self.shift[buf]
         self.pairs[buf].wait()
-
-        def add(j):
-            rows = pl.ds(start + j * 16, 16)
-            r.tiles[buf][rows] = (
-                r.tiles[buf][rows].astype(F32) + r.sums[buf][rows].astype(F32)
-            ).astype(BF)
-
-        loop(half // 16, add)
-
-    def rs_start(self, g, stage):
-        r, at = self.r, self.at
-        buf, start, tiles, axes = GROUPS[g]
-        axis = axes[stage]
-        count = extent(axis)
-        for a in axes[:stage]:
-            tiles //= extent(a)
-        if stage == 0:
-            self.base[g] = self.shift[buf] + start
-        part = tiles // count
+        self.add(self.r.tiles[buf], self.shift[buf], HALF[buf], [self.r.sums[buf].at[pl.ds(self.shift[buf], HALF[buf])]])
+
+    def add(self, to, start, count, others, src=None):
+        src = to if src is None else src
+        block = max(b for b in range(1, 17) if count % b == 0)
+
+        def some(i):
+            mine = pl.ds(start + i * block, block)
+            rows = pl.ds(i * block, block)
+            total = src[mine].astype(F32)
+            for o in others:
+                total = total + o[rows].astype(F32)
+            to[mine] = total.astype(BF)
+
+        loop(count // block, some)
+
+    def send(self, g, sem, src, dst, dev):
+        rcopy(src, dst, self.r.rs.at[g, sem], self.r.rr.at[g, sem], dev).start()
+
+    def wait(self, g, sem, like):
+        arrived(like, self.r.rs.at[g, sem], self.r.rr.at[g, sem], self.at)
+
+    def ring(self, g):
+        buf, start, tiles, axis, _ = GROUPS[g]
+        part = tiles // 4
+        first = self.shift[buf] + start
+        quarters = [first + (self.at[axis] + i) % 4 * part for i in range(4)]
+        right, left = peer_on(self.at, axis, 1)[0], peer_on(self.at, axis, 3)[0]
+        return buf, part, quarters, right, left
+
+    def ring_start(self, g):
+        buf, part, (_, to_right, far, to_left), right, left = self.ring(g)
+        half = part // 2
+        tiles, opp, near = self.r.tiles[buf], self.r.recv[g, "opp"], self.r.recv[g, "near"]
+        self.send(g, 0, tiles.at[pl.ds(far, half)], opp.at[0], right)
+        self.send(g, 0, tiles.at[pl.ds(far + half, half)], opp.at[1], left)
+        low, high = pl.ds(0, half), pl.ds(half, half)
+        self.send(g, 1, tiles.at[pl.ds(to_right + half, half)], near.at[0, high], right)
+        self.send(g, 1, tiles.at[pl.ds(to_left, half)], near.at[1, low], left)
+
+    def ring_relay(self, g):
+        buf, part, (_, to_right, _, to_left), right, left = self.ring(g)
+        half = part // 2
+        tiles, opp, near = self.r.tiles[buf], self.r.recv[g, "opp"], self.r.recv[g, "near"]
+        self.wait(g, 0, opp)
+        low, high = pl.ds(0, half), pl.ds(half, half)
+        self.add(tiles, to_right, half, [opp.at[0]])
+        self.send(g, 1, tiles.at[pl.ds(to_right, half)], near.at[0, low], right)
+        self.add(tiles, to_left + half, half, [opp.at[1]])
+        self.send(g, 1, tiles.at[pl.ds(to_left + half, half)], near.at[1, high], left)
+
+    def plane_start(self, g):
+        buf, part, quarters, _, _ = self.ring(g)
+        near = self.r.recv[g, "near"]
+        self.wait(g, 1, near)
+        self.add(self.r.tiles[buf], quarters[0], part, [near.at[0], near.at[1]])
+        plane = GROUPS[g][4]
+        small = part // extent(plane)
+        for i in range(1, extent(plane)):
+            dev, q = peer_on(self.at, plane, i)
+            src = self.r.tiles[buf].at[pl.ds(quarters[0] + q * small, small)]
+            self.send(g, 2, src, self.r.recv[g, "plane"].at[i - 1], dev)
+
+    def gather_start(self, g):
+        buf, part, quarters, _, _ = self.ring(g)
+        plane = GROUPS[g][4]
+        count = extent(plane)
+        small = part // count
+        got = self.r.recv[g, "plane"]
+        self.wait(g, 2, got)
+        here = quarters[0] + index_on(self.at, plane) * small
+        self.add(
+            self.r.sums[buf], here, small, [got.at[i] for i in range(count - 1)], self.r.tiles[buf]
+        )
+        mine = self.r.sums[buf].at[pl.ds(here, small)]
         for i in range(1, count):
-            dev, q = peer_on(at, axis, i)
-            rcopy(
-                r.tiles[buf].at[pl.ds(self.base[g] + q * part, part)],
-                r.recv[g, stage].at[i - 1],
-                r.rs.at[g, stage],
-                r.rr.at[g, stage],
-                dev,
-            ).start()
-        self.part[g] = part
-
-    def rs_end(self, g, stage):
+            self.send(g, 3, mine, mine, peer_on(self.at, plane, i)[0])
+
+    def gather_ring(self, g):
+        buf, part, quarters, right, left = self.ring(g)
+        sums = self.r.sums[buf]
+        count = extent(GROUPS[g][4])
+        self.wait(g, 3, sums.at[pl.ds(0, (count - 1) * (part // count))])
+        mine = sums.at[pl.ds(quarters[0], part)]
+        self.send(g, 4, mine, mine, right)
+        self.send(g, 4, mine, mine, left)
+        self.share(g, 0)
+
+    def gather_relay(self, g):
+        buf, part, (_, of_right, _, of_left), right, left = self.ring(g)
+        half = part // 2
+        sums = self.r.sums[buf]
+        self.wait(g, 4, sums.at[pl.ds(0, 2 * part)])
+        low = sums.at[pl.ds(of_left, half)]
+        self.send(g, 5, low, low, right)
+        high = sums.at[pl.ds(of_right + half, half)]
+        self.send(g, 5, high, high, left)
+        self.share(g, 1)
+        self.share(g, 3)
+
+    def gather_end(self, g):
+        buf, part, _, _, _ = self.ring(g)
+        self.wait(g, 5, self.r.sums[buf].at[pl.ds(0, part)])
+        self.share(g, 2)
+
+    def share(self, g, i):
+        buf, part, quarters, _, _ = self.ring(g)
         r = self.r
-        buf, _, _, axes = GROUPS[g]
-        part = self.part[g]
-        got = r.recv[g, stage]
-        arrived(got, r.rs.at[g, stage], r.rr.at[g, stage], self.at)
-        here = self.base[g] + index_on(self.at, axes[stage]) * part
-        block = max(b for b in range(1, 17) if part % b == 0)
-
-        def add(i):
-            rows = pl.ds(i * block, block)
-            mine = pl.ds(here + i * block, block)
-            total = r.tiles[buf][mine].astype(F32)
-            for j in range(extent(axes[stage]) - 1):
-                total = total + r.recv[g, stage][j, rows].astype(F32)
-            to = r.sums if stage == 1 else r.tiles
-            to[buf][mine] = total.astype(BF)
-
-        loop(part // block, add)
-        self.base[g] = here
-
-    def ag_start(self, g, stage):
-        r = self.r
-        buf, _, _, axes = GROUPS[g]
-        rows = pl.ds(self.base[g], self.part[g])
-        for i in range(1, extent(axes[stage])):
-            dev, _ = peer_on(self.at, axes[stage], i)
-            rcopy(
-                r.sums[buf].at[rows],
-                r.sums[buf].at[rows],
-                r.gs.at[g, stage],
-                r.gr.at[g, stage],
-                dev,
-            ).start()
-
-    def ag_end(self, g, stage):
-        r = self.r
-        buf, _, _, axes = GROUPS[g]
-        axis = axes[stage]
-        count = (extent(axis) - 1) * self.part[g]
-        arrived(r.sums[buf].at[pl.ds(0, count)], r.gs.at[g, stage], r.gr.at[g, stage], self.at)
-        self.base[g] = self.base[g] - index_on(self.at, axis) * self.part[g]
-        self.part[g] = self.part[g] * extent(axis)
-
-    def share_start(self, g):
-        r = self.r
-        buf, start, tiles, _ = GROUPS[g]
-        if buf < 4:
-            rows = pl.ds(self.shift[buf] + start, tiles)
-            rcopy(
-                r.sums[buf].at[rows],
-                r.sums[buf].at[rows],
-                r.fs.at[buf],
-                r.fr.at[buf],
-                core_dev(self.at),
-            ).start()
+        if buf < 5:
+            rows = r.sums[buf].at[pl.ds(quarters[i], part)]
+            rcopy(rows, rows, r.fs.at[buf], r.fr.at[buf], core_dev(self.at)).start()
 
     def share_end(self, buf):
         r = self.r
@@ -417,8 +436,8 @@
         setattr(r, name, ref)
     for (name, _, _), ref in zip(SCRATCH, take(len(SCRATCH))):
         setattr(r, name, ref)
-    r.tiles = take(5)
-    r.sums = take(5)
+    r.tiles = take(6)
+    r.sums = take(6)
     r.recv = {}
     for (key, _), ref in zip(recv_shapes(), take(len(recv_shapes()))):
         r.recv[key] = ref
@@ -444,8 +463,9 @@
 
     copies = []
 
-    def leave(src, name):
-        cp = pltpu.make_async_copy(src, outs[name], r.out.at[len(copies)])
+    def leave(src, name, rows=None):
+        dst = outs[name] if rows is None else outs[name].at[rows]
+        cp = pltpu.make_async_copy(src, dst, r.out.at[len(copies)])
         cp.start()
         copies.append(cp)
 
@@ -547,7 +567,7 @@
         for i, b in enumerate(blocks):
             value = dot(r.one_t[...], r.zp[:, b])
             if w == 1 and i == 2:
-                put(r.tiles[3], T_ZERO2, value)
+                put(r.tiles[4], T_ZERO2, value)
             else:
                 put(to, T_ZERO[w] + i * 48, value)
 
@@ -578,34 +598,38 @@
     sums = Sums(r, at)
     r.flipped[...] = flip(r.hidden[...])
     for i, b in enumerate(blocks):
-        value = dot(r.flipped[...], r.gto[:, b])
-        if i < 2:
-            put(r.tiles[0], T_HID + i * 96, value)
+        put(r.tiles[0], T_HID + i * 96, dot(r.flipped[...], r.gto[:, b]))
+    r.flipped[...] = flip(r.tin[...])
+    put(r.tiles[0], T_IN0, dot(r.flipped[...], r.ffn[:, :256]))
+    sums.core_start(0)
+    for i in range(1, 6):
+        value = dot(r.flipped[...], r.ffn[:, i * 256 : (i + 1) * 256])
+        if i < 5:
+            put(r.tiles[1], T_IN + (i - 1) * 96, value)
         else:
-            put(r.tiles[0], T_HID + 192, value[:, :128])
-            put(r.tiles[0], T_HID + 240, value[:256, 128:])
-            put(r.tiles[2], T_HID2, value[256:, 128:])
-    r.flipped[...] = flip(r.tin[...])
-    for i in range(6):
-        put(r.tiles[0], T_IN + i * 96, dot(r.flipped[...], r.ffn[:, i * 256 : (i + 1) * 256]))
-    sums.core_start(0)
+            put(r.tiles[1], T_IN + 384, value[:, :128])
+            put(r.tiles[1], T_IN + 432, value[:256, 128:])
+            put(r.tiles[3], T_IN2, value[256:, 128:])
+    sums.core_start(1)
+    sums.core_end(0)
+    sums.ring_start(0)
     for b in blocks:
         branch_out(1, b, dot(r.hidden[...], r.hid[:, b]))
     for b in blocks:
         branch_in(
             1, b, dot_t(r.ffn[:, :D], r.win[0, b, :]) + dot_t(r.ffn[:, D:], r.win[1, b, :])
         )
-    conditioned(1, r.tiles[1])
-    sums.core_start(1)
-    sums.core_end(0)
-    sums.rs_start(0, 0)
-    sums.rs_start(1, 0)
+    sums.core_end(1)
+    sums.ring_start(1)
+    conditioned(1, r.tiles[2])
+    sums.core_start(2)
     need("ada0", "zero0")
     modulation(0)
     branch_start(0, r.ain, r.gao)
-    sums.core_end(1)
-    sums.rs_start(2, 0)
-    sums.rs_start(3, 0)
+    sums.core_end(2)
+    for g in (2, 3, 4):
+        sums.ring_start(g)
+    sums.ring_relay(0)
 
     need("wq", "qb", "wout")
     r.qkv[0] = (dot(r.ain[...], r.wq[0]) + r.qb[...].astype(F32).reshape(1, 384)).astype(BF)
@@ -615,6 +639,7 @@
     r.ggat[...] = dot_t(r.gao[...], r.wout[...])
     r.gatt[...] = (r.ggat[...] * r.gsig[...]).astype(BF)
     conditioning_back(1)
+    sums.ring_relay(1)
     arrived(r.bias.at[pl.ds(0, NS - 1)], r.bs.at[0], r.br.at[0], at)
     wt_copy.wait()
     r.acc[...] = jnp.zeros(r.acc.shape, F32)
@@ -656,6 +681,13 @@
             else:
                 for s in range(NS):
                     r.gb[1, s % 4 * 8 + s // 8 * 2 + s // 4 % 2, rows, :] = two[s]
+        if h == 1:
+            for g in (2, 3, 4):
+                sums.ring_relay(g)
+        if h == 4:
+            sums.plane_start(0)
+        if h == 6:
+            sums.plane_start(1)
     for half, axis in enumerate("zx"):
         for i in range(1, 4):
             dev, q = peer_on(at, axis, i)
@@ -682,14 +714,18 @@
     r.mixs[...] = r.mixf[...].astype(BF)
     mix_copy = rcopy(r.mixs, r.mixr, r.hs.at[1], r.hr.at[1], head_dev(at))
     mix_copy.start()
+    for g in (2, 3, 4):
+        sums.plane_start(g)
     r.flipped[:384] = flip(gated)
     for i, b in enumerate(blocks):
-        put(r.tiles[2], T_OUT + i * 48, dot(r.flipped[:384], r.gao[:, b]))
+        put(r.tiles[3], T_OUT + i * 48, dot(r.flipped[:384], r.gao[:, b]))
     r.flipped[...] = flip(r.ain[...])
     for i in range(6):
-        put(r.tiles[2], T_QKVG + i * 96, dot(r.flipped[...], r.gheads[:, i * 256 : (i + 1) * 256]))
-    r.tiles[2][T_WPAD:] = jnp.zeros((TILES[2] - T_WPAD, 16, 128), BF)
-    sums.core_start(2)
+        put(r.tiles[3], T_QKVG + i * 96, dot(r.flipped[...], r.gheads[:, i * 256 : (i + 1) * 256]))
+    r.tiles[3][T_WPAD:] = jnp.zeros((TILES[3] - T_WPAD, 16, 128), BF)
+    sums.core_start(3)
+    for g in (0, 1):
+        sums.gather_start(g)
     for b in blocks:
         total = dot_t(r.gheads[:, :384], r.wq[0, b, :])
         for k in range(1, 4):
@@ -698,17 +734,25 @@
     r.acts[...] = r.actf[...].astype(BF)
     act_copy = rcopy(r.acts, r.actr, r.hs.at[2], r.hr.at[2], head_dev(at))
     act_copy.start()
-    conditioned(0, r.tiles[3])
+    conditioned(0, r.tiles[4])
     conditioning_back(0)
-    r.tiles[3][T_SMALL:T_APAD] = r.small_a[...].astype(BF).reshape(2, 16, 128)
-    r.tiles[3][T_APAD:] = jnp.zeros((TILES[3] - T_APAD, 16, 128), BF)
-    sums.core_start(3)
-    for g in FIRST:
-        sums.rs_end(g, 0)
-        sums.rs_start(g, 1)
-    sums.core_end(2)
-    sums.rs_start(4, 0)
-    sums.rs_start(5, 0)
+    r.tiles[4][T_SMALL:T_APAD] = r.small_a[...].astype(BF).reshape(2, 16, 128)
+    r.tiles[4][T_APAD:] = jnp.zeros((TILES[4] - T_APAD, 16, 128), BF)
+    sums.core_start(4)
+    sums.core_end(3)
+    for g in (5, 6):
+        sums.ring_start(g)
+    grad_single = norm_back(r.gsh[...], r.shat[...], r.sinv[:, :1]) + r.zterm[...]
+    put(r.tiles[5], 0, grad_single)
+    r.tiles[5][48:] = jnp.zeros((TILES[5] - 48, 16, 128), BF)
+    sums.ring_start(10)
+    for g in (2, 3, 4):
+        sums.gather_start(g)
+    for g in (0, 1):
+        sums.gather_ring(g)
+    sums.core_end(4)
+    for g in (7, 8, 9):
+        sums.ring_start(g)
     for half in range(2):
         arrived(r.gb1.at[half], r.b1s.at[half], r.b1r.at[half], at)
         own = pl.ds(at["zx"[half]] * 8, 8)
@@ -725,16 +769,14 @@
                 r.b2r.at[half],
                 dev,
             ).start()
-    sums.core_end(3)
-    for g in (6, 7, 8):
-        sums.rs_start(g, 0)
-    grad_single = norm_back(r.gsh[...], r.shat[...], r.sinv[:, :1]) + r.zterm[...]
-    put(r.tiles[4], 0, grad_single)
-    r.tiles[4][48:] = jnp.zeros((TILES[4] - 48, 16, 128), BF)
-    sums.rs_start(9, 0)
-    for g in FIRST:
-        sums.rs_end(g, 1)
-        sums.ag_start(g, 1)
+    for g in (5, 6, 10):
+        sums.ring_relay(g)
+    for g in (2, 3, 4):
+        sums.gather_ring(g)
+    for g in (7, 8, 9):
+        sums.ring_relay(g)
+    for g in (0, 1):
+        sums.gather_relay(g)
     places = (at["z"] * 8 + at["l"] * 4 + at["x"], at["x"] * 8 + at["z"] * 2 + at["l"])
     for half in range(2):
         arrived(r.gb2.at[half], r.b2s.at[half], r.b2r.at[half], at)
@@ -753,9 +795,12 @@
 
     loop(16, last_mix)
     leave(r.hidden, "mixed_o")
-    for g in FIRST:
-        sums.ag_end(g, 1)
-        sums.ag_start(g, 0)
+    for g in (5, 6):
+        sums.plane_start(g)
+    for g in (2, 3, 4):
+        sums.gather_relay(g)
+    for g in (7, 8, 9, 10):
+        sums.plane_start(g)
 
     rows_copy.wait()
     r.rows[...] = r.gball[hd].astype(F32).reshape(8, 8, N)
@@ -791,11 +836,12 @@
         r.small_w[...] = total
 
     small_start(0)
-    for g in SECOND:
-        sums.rs_end(g, 0)
-        sums.rs_start(g, 1)
+    for g in FIRST:
+        sums.gather_end(g)
     small_end(0)
     small_start(1)
+    for g in SECOND:
+        sums.gather_start(g)
     act_copy.wait()
 
     def last_act(i):
@@ -809,28 +855,26 @@
     small_end(1)
     small_start(2)
     for g in SECOND:
-        sums.rs_end(g, 1)
-        sums.ag_start(g, 1)
+        sums.gather_ring(g)
+    for b in (0, 1, 2):
+        sums.share_end(b)
+        leave(r.sums[b], "sum%d" % b)
     small_end(2)
     small_start(3)
-    for g in FIRST:
-        sums.ag_end(g, 0)
-        sums.share_start(g)
     for g in SECOND:
-        sums.ag_end(g, 1)
-        sums.ag_start(g, 0)
+        sums.gather_relay(g)
     small_end(3)
     leave(r.small_w, "small_o")
-    for b in (0, 1):
+    for g in SECOND:
+        sums.gather_end(g)
+    leave(r.sums[5], "sum5")
+    own = [pl.ds(sums.shift[b], HALF[b]) for b in range(5)]
+    other = [pl.ds((1 - at["c"]) * HALF[b], HALF[b]) for b in range(5)]
+    for b in (3, 4):
+        leave(r.sums[b].at[own[b]], "sum%d" % b, own[b])
+    for b in (3, 4):
         sums.share_end(b)
-        leave(r.sums[b], "sum%d" % b)
-    for g in SECOND:
-        sums.ag_end(g, 0)
-        sums.share_start(g)
-    leave(r.sums[4], "sum4")
-    for b in (2, 3):
-        sums.share_end(b)
-        leave(r.sums[b], "sum%d" % b)
+        leave(r.sums[b].at[other[b]], "sum%d" % b, other[b])
     for cp in copies:
         cp.wait()
 
@@ -884,15 +928,15 @@
         del refs[:count]
         return got
 
-    ins = take(9)
+    ins = take(10)
     outs = take(3 + len(FINAL))
-    held = take(9)
+    held = take(10)
     f = Refs()
     for (name, _), ref in zip(FINAL, take(len(FINAL))):
         setattr(f, name, ref)
     in_sem, out_sem = take(2)
     loads = []
-    for i in range(9):
+    for i in range(10):
         cp = pltpu.make_async_copy(ins[i], held[i], in_sem.at[i])
         cp.start()
         loads.append(cp)
@@ -908,58 +952,63 @@
         return held[b][pl.ds(start, rows // 16)].astype(F32).reshape(rows, 128)
 
     cols = [slice(j * 128, (j + 1) * 128) for j in range(12)]
-    loads[0].wait()
-    for k in range(2):
-        for j in range(6):
-            f.win[:, k, cols[j]] = get(0, T_IN + (k * 6 + j) * 48, 768)
-    leave("win")
     for i in range(3):
-        loads[6 + i].wait()
-        cp = pltpu.make_async_copy(held[6 + i], outs[i], out_sem.at[i])
+        loads[7 + i].wait()
+        cp = pltpu.make_async_copy(held[7 + i], outs[i], out_sem.at[i])
         cp.start()
         copies.append(cp)
-    loads[2].wait()
-    for j in range(5):
+    loads[0].wait()
+    for j in range(6):
         f.hid[:, cols[j]] = get(0, T_HID + j * 48, 768)
-    f.hid[:256, cols[5]] = get(0, T_HID + 240, 256)
-    f.hid[256:, cols[5]] = get(2, T_HID2, 512)
     leave("hid")
+    loads[3].wait()
     for k in range(4):
         for j in range(3):
-            f.qkvg[:, k, cols[j]] = get(2, T_QKVG + (k * 3 + j) * 48, 768)
+            f.qkvg[:, k, cols[j]] = get(3, T_QKVG + (k * 3 + j) * 48, 768)
     leave("qkvg")
     for j in range(6):
-        f.wout[:, cols[j]] = get(2, T_OUT + j * 24, 384)
+        f.wout[:, cols[j]] = get(3, T_OUT + j * 24, 384)
     leave("wout")
     loads[1].wait()
-    loads[3].wait()
+    for i in range(12):
+        k, j = i // 6, i % 6
+        if i < 2:
+            f.win[:, k, cols[j]] = get(0, T_IN0 + i * 48, 768)
+        elif i < 11:
+            f.win[:, k, cols[j]] = get(1, T_IN + (i - 2) * 48, 768)
+        else:
+            f.win[:256, k, cols[j]] = get(1, T_IN + 432, 256)
+            f.win[256:, k, cols[j]] = get(3, T_IN2, 512)
+    leave("win")
+    loads[2].wait()
+    loads[4].wait()
     for w in range(2):
         for j in range(12):
-            f.ada[w, :, cols[j]] = get(3 - 2 * w, T_ADA[w] + j * 24, 384)
+            f.ada[w, :, cols[j]] = get(4 - 2 * w, T_ADA[w] + j * 24, 384)
     leave("ada")
     for w in range(2):
         for j in range(6):
             if w == 1 and j >= 4:
-                f.zero[w, :, cols[j]] = get(3, T_ZERO2 + (j - 4) * 24, 384)
+                f.zero[w, :, cols[j]] = get(4, T_ZERO2 + (j - 4) * 24, 384)
             else:
-                f.zero[w, :, cols[j]] = get(3 - 2 * w, T_ZERO[w] + j * 24, 384)
+                f.zero[w, :, cols[j]] = get(4 - 2 * w, T_ZERO[w] + j * 24, 384)
     leave("zero")
-    loads[4].wait()
+    loads[5].wait()
     for j in range(3):
-        f.single[:, cols[j]] = get(4, j * 16, 256)
+        f.single[:, cols[j]] = get(5, j * 16, 256)
     leave("single")
-    small = held[3][T_SMALL:T_APAD].astype(F32).reshape(32, 128)
+    small = held[4][T_SMALL:T_APAD].astype(F32).reshape(32, 128)
     for w in range(2):
         for j in range(6):
             f.adab[w : w + 1, cols[j]] = small[6 * w + j : 6 * w + j + 1]
             f.zerob[w : w + 1, cols[j]] = small[12 + 6 * w + j : 13 + 6 * w + j]
         for j in range(3):
             f.gain[w : w + 1, cols[j]] = small[24 + 3 * w + j : 25 + 3 * w + j]
-    loads[5].wait()
-    f.wt[...] = held[5][:8]
-    f.pgain[...] = held[5][8]
+    loads[6].wait()
+    f.wt[...] = held[6][:8]
+    f.pgain[...] = held[6][8]
     for j in range(3):
-        f.qb[cols[j]] = held[5][9 + j]
+        f.qb[cols[j]] = held[6][9 + j]
     for name in ("adab", "zerob", "gain", "wt", "pgain", "qb"):
         leave(name)
     for cp in copies:
@@ -976,8 +1025,8 @@
         out_specs=[pl.BlockSpec(memory_space=pl.ANY)] * len(shapes),
         scratch_shapes=[pltpu.VMEM(a.shape, a.dtype) for a in args]
         + [pltpu.VMEM(shape, F32) for _, shape in FINAL]
-        + [pltpu.SemaphoreType.DMA((9,)), pltpu.SemaphoreType.DMA((len(shapes),))],
-        compiler_params=pltpu.CompilerParams(vmem_limit_bytes=48 * 2**20),
+        + [pltpu.SemaphoreType.DMA((10,)), pltpu.SemaphoreType.DMA((len(shapes),))],
+        compiler_params=pltpu.CompilerParams(vmem_limit_bytes=63 * 2**20),
         name="finish",
     )(*args)
 

time: 142 us -> 128 us (0.901)
  local copies, waits for them, and re-layouts: 13.2 us -> 5.23 us
  Pallas kernels: 127 us -> 122 us
    unnamed x18 -> x4, local copies, waits for them, and re-layouts: 13.2 us -> 5.23 us
    pallas_call x1, Pallas kernels: 114 us -> 107 us  [mega(): pl.pallas_call(mega_kernel, out_shape=tuple((whole(shape, dtype) for _, s...]
    pallas_call x1, Pallas kernels: 12.3 us -> 14.7 us  [finish(): pl.pallas_call(finish_kernel, out_shape=tuple(shapes), in_specs=[pl.Block...]
where the time goes in v3:
time: 128 us
  Pallas kernels  122 us (95%)
  local copies, waits for them, and re-layouts  5.23 us (4%)
  between operations  1.49 us (1%)
    pallas_call x1, Pallas kernels, mega(): pl.pallas_call(mega_kernel, out_shape=tuple((whole(shape, dtype) for _, s...  107 us
    pallas_call x1, Pallas kernels, finish(): pl.pallas_call(finish_kernel, out_shape=tuple(shapes), in_specs=[pl.Block...  14.7 us
    unnamed x4, local copies, waits for them, and re-layouts  5.23 us

profile of v3, /device:TPU:1, one launch (start us, length us, event | category | flops | bytes accessed | tf_op | source)
XLA Modules:
  0.0 128.3 jit_solution(9436462133866675111)
XLA Ops:
  1.3 0.0 copy-start
  1.3 3.5 %copy.37 = bf16[768,4,384]{2,0,1:T(8,128)(2,1)} copy(bf16[768,4,384]{2,1,0:T(4,128)(2,1)} %param.26) | data formatting | bytes 4718592 | tf_op args[9]
  4.8 0.0 copy-done
  4.8 1.7 %copy.38 = bf16[768,2,768]{2,0,1:T(8,128)(2,1)} copy(bf16[768,2,768]{2,1,0:T(2,128)(2,1)S(1)} %copy-done) | data formatting | bytes 4718592 | tf_op args[12]
  6.5 106.9 %block.1 = (bf16[384,16,128]{2,1,0:T(8,128)(2,1)}, bf16[448,16,128]{2,1,0:T(8,128)(2,1)}, bf16[384,16,128]{2,1,0:T(8,128)(2,1)}, bf16[768,16,128]{2,1,0:T(8,128)...) custom-call(s32[1]{0:T(128)S(6)} %copy.39.refs_0_, ...), custom_call_target="tpu_custom_call" | custom-call | tf_op jit(solution)/shard_map/block/pallas_call | solution.py:887
  113.5 14.7 %finish.1 = (bf16[256,768]{1,0:T(8,128)(2,1)}, f32[256,768]{1,0:T(8,128)}, f32[8,256,128]{2,1,0:T(8,128)}, f32[768,4,384]{2,1,0:T(4,128)}, f32[768,2,768]{2,1,0:...) custom-call(bf16[384,16,128]{2,1,0:T(8,128)(2,1)} %get-tuple-element, ...), custom_call_target="tpu_custom_call" | custom-call | tf_op jit(solution)/shard_map/finish/pallas_call | solution.py:1021
Async XLA Ops:
  1.3 3.5 %copy-start = (bf16[768,2,768]{2,1,0:T(2,128)(2,1)S(1)}, bf16[768,2,768]{2,1,0:T(2,128)(2,1)}, u32[]{:S(2)}) copy-start(bf16[768,2,768]{2,1,0:T(2,128)(2,1)} %param.29) | copy-start | bytes 7077892

commit v4 on v3

--- a/solution.py
+++ b/solution.py
@@ -164,7 +164,7 @@
 T_HID, T_IN0, T_IN = 0, 288, 0
 T_ADA, T_ZERO = (0, 0), (288, 288)
 T_QKVG, T_OUT, T_IN2, T_WPAD = 0, 576, 720, 752
-T_ZERO2, T_SMALL, T_APAD = 432, 480, 482
+T_ZERO2, T_APAD = 432, 480
 
 INPUTS = (
     ("pair", (8, 256, 128)),
@@ -197,7 +197,6 @@
     ("shat", (N, 384), F32),
     ("sinv", (N, 128), F32),
     ("s_hi", (2, N, 384), BF),
-    ("s_lo", (2, N, 384), BF),
     ("s_t", (2, 384, N), BF),
     ("one_t", (384, N), BF),
     ("mg", (2, N, D), F32),
@@ -210,8 +209,8 @@
     ("gto", (N, D), BF),
     ("hidden", (N, D), BF),
     ("ffn", (N, 2 * D), BF),
-    ("pre", (N, 2 * D), BF),
-    ("zp", (N, D), BF),
+    ("pre", (2, N, 2 * D), BF),
+    ("zp", (2, N, D), BF),
     ("mixf", (N, D), F32),
     ("actf", (N, D), F32),
     ("mixs", (N, D), BF),
@@ -224,18 +223,21 @@
     ("gsig", (N, 384), F32),
     ("ggat", (N, 384), F32),
     ("gatt", (N, 384), BF),
-    ("acc", (4, N, 384), F32),
+    ("acc", (2, N, 384), F32),
+    ("qt", (384, N), BF),
+    ("gt", (384, N), BF),
+    ("dkt", (384, N), F32),
+    ("dvt", (384, N), F32),
     ("gheads", (N, 1536), BF),
     ("flipped", (D, N), BF),
     ("held", (NS, 8, N), F32),
-    ("small_a", (32, 128), F32),
-    ("small_w", (16, 128), F32),
+    ("small", (48, 128), F32),
     ("gb", (2, NS, 32, N), BF),
     ("gb1", (2, 3, 8, 32, N), BF),
     ("gb2", (2, 7, 32, N), BF),
     ("gball", (2, 64, N), BF),
     ("gpair", (8, N, 128), F32),
-    ("slot", (4, 4, 16, 128), F32),
+    ("slot", (5, 4, 48, 128), F32),
 )
 SEMS = (
     ("ld", (len(LOADS),)),
@@ -254,11 +256,11 @@
     ("b2s", (2,)),
     ("b2r", (2,)),
     ("out", (12,)),
-    ("ss", (4,)),
-    ("sr", (4,)),
+    ("ss", (5,)),
+    ("sr", (5,)),
 )
 OUTPUTS = tuple(("sum%d" % i, (t, 16, 128), BF) for i, t in enumerate(TILES)) + (
-    ("small_o", (16, 128), F32),
+    ("small_o", (48, 128), F32),
     ("mixed_o", (N, D), BF),
     ("act_o", (N, D), F32),
     ("pair_o", (8, N, 128), F32),
@@ -446,6 +448,11 @@
 
     at = place()
     me, hd = at["s"], at["h"]
+    bar = pltpu.get_barrier_semaphore()
+    greet_samp(at, bar)
+    cross = {"cplx": at["c"], "samp": at["z"] * 8 + (1 - at["l"]) * 4 + at["x"], "head": 1 - hd}
+    for dev in (head_dev(at), core_dev(at), cross):
+        signal(bar, dev)
     blocks = [slice(i * 256, (i + 1) * 256) for i in range(3)]
     loads = {}
     places = {name: i for i, (name, _) in enumerate(INPUTS)}
@@ -478,11 +485,6 @@
         r.rows[:, i, :] = dot_t(wt, (normed * pgain).astype(BF))
     r.part[...] = r.rows[...].reshape(64, N).astype(BF)
     r.bias[me] = r.part[...]
-    bar = pltpu.get_barrier_semaphore()
-    greet_samp(at, bar)
-    cross = {"cplx": at["c"], "samp": at["z"] * 8 + (1 - at["l"]) * 4 + at["x"], "head": 1 - hd}
-    for dev in (head_dev(at), core_dev(at), cross):
-        signal(bar, dev)
     pl.semaphore_wait(bar, NS + 2)
 
     def bias_copy(i):
@@ -494,8 +496,7 @@
     wt_copy = rcopy(r.wall.at[hd], r.wall.at[hd], r.hs.at[0], r.hr.at[0], head_dev(at))
     wt_copy.start()
 
-    r.small_a[...] = jnp.zeros(r.small_a.shape, F32)
-    r.small_w[...] = jnp.zeros(r.small_w.shape, F32)
+    r.small[...] = jnp.zeros(r.small.shape, F32)
     need("single", "gain")
     gains = r.gain[...].astype(F32)
 
@@ -505,10 +506,7 @@
         r.shat[rows] = normed
         r.sinv[rows] = jnp.broadcast_to(inv, (32, 128))
         for w in range(2):
-            scaled = normed * gains[w : w + 1]
-            high = scaled.astype(BF)
-            r.s_hi[w, rows] = high
-            r.s_lo[w, rows] = (scaled - high.astype(F32)).astype(BF)
+            r.s_hi[w, rows] = (normed * gains[w : w + 1]).astype(BF)
 
     loop(N // 32, cond)
 
@@ -517,9 +515,8 @@
         zerob = r.zerob[...].astype(F32)
         for b in blocks:
             later = slice(D + b.start, D + b.stop)
-            pre_gate = dot(r.s_hi[w], r.ada[w, :, b]) + dot(r.s_lo[w], r.ada[w, :, b])
-            r.mg[w, :, b] = sigmoid(pre_gate + adab[w : w + 1, b])
-            r.ms[:, b] = dot(r.s_hi[w], r.ada[w, :, later]) + dot(r.s_lo[w], r.ada[w, :, later])
+            r.mg[w, :, b] = sigmoid(dot(r.s_hi[w], r.ada[w, :, b]) + adab[w : w + 1, b])
+            r.ms[:, b] = dot(r.s_hi[w], r.ada[w, :, later])
             r.zg[w, :, b] = sigmoid(dot(r.single[...], r.zero[w, :, b]) + zerob[w : w + 1, b])
 
     def branch_start(w, x_ref, g_ref):
@@ -545,27 +542,27 @@
         share = gate * part
         r.mixf[:, b] = share if w == 1 else r.mixf[:, b] + share
         grad = r.cot[:, b].astype(F32) * share * (1.0 - gate)
-        r.zp[:, b] = grad.astype(BF)
+        r.zp[w, :, b] = grad.astype(BF)
         for j in range(2):
-            row = 12 + 6 * w + b.start // 128 + j
-            r.small_a[row : row + 1] = jnp.sum(grad[:, j * 128 : (j + 1) * 128], 0, keepdims=True)
+            row = 28 + 6 * w + b.start // 128 + j
+            r.small[row : row + 1] = jnp.sum(grad[:, j * 128 : (j + 1) * 128], 0, keepdims=True)
 
     def branch_in(w, b, grad_in):
         gate = r.mg[w, :, b]
         share = gate * grad_in
         r.actf[:, b] = share if w == 1 else r.actf[:, b] + share
         grad = share * r.hat[:, b] * (1.0 - gate)
-        r.pre[:, b] = grad.astype(BF)
-        r.pre[:, D + b.start : D + b.stop] = grad_in.astype(BF)
+        r.pre[w, :, b] = grad.astype(BF)
+        r.pre[w, :, D + b.start : D + b.stop] = grad_in.astype(BF)
         for j in range(2):
-            row = 6 * w + b.start // 128 + j
-            r.small_a[row : row + 1] = jnp.sum(grad[:, j * 128 : (j + 1) * 128], 0, keepdims=True)
+            row = 16 + 6 * w + b.start // 128 + j
+            r.small[row : row + 1] = jnp.sum(grad[:, j * 128 : (j + 1) * 128], 0, keepdims=True)
 
     def conditioned(w, to):
         for i in range(6):
-            put(to, T_ADA[w] + i * 48, dot(r.s_t[w], r.pre[:, i * 256 : (i + 1) * 256]))
+            put(to, T_ADA[w] + i * 48, dot(r.s_t[w], r.pre[w, :, i * 256 : (i + 1) * 256]))
         for i, b in enumerate(blocks):
-            value = dot(r.one_t[...], r.zp[:, b])
+            value = dot(r.one_t[...], r.zp[w, :, b])
             if w == 1 and i == 2:
                 put(r.tiles[4], T_ZERO2, value)
             else:
@@ -574,11 +571,11 @@
     def conditioning_back(w):
         for j in range(3):
             b = slice(j * 128, (j + 1) * 128)
-            scaled = dot_t(r.pre[...], r.ada[w, b, :])
-            row = 24 + 3 * w + j
-            r.small_a[row : row + 1] = jnp.sum(scaled * r.shat[:, b], 0, keepdims=True)
+            scaled = dot_t(r.pre[w], r.ada[w, b, :])
+            row = 40 + 3 * w + j
+            r.small[row : row + 1] = jnp.sum(scaled * r.shat[:, b], 0, keepdims=True)
             share = scaled * gains[w : w + 1, b]
-            through = dot_t(r.zp[...], r.zero[w, b, :])
+            through = dot_t(r.zp[w], r.zero[w, b, :])
             r.gsh[:, b] = share if w == 1 else r.gsh[:, b] + share
             r.zterm[:, b] = through if w == 1 else r.zterm[:, b] + through
 
@@ -637,8 +634,10 @@
     r.qkv[2] = dot(r.ain[...], r.wq[2]).astype(BF)
     r.gsig[...] = sigmoid(dot(r.ain[...], r.wq[3]))
     r.ggat[...] = dot_t(r.gao[...], r.wout[...])
-    r.gatt[...] = (r.ggat[...] * r.gsig[...]).astype(BF)
-    conditioning_back(1)
+    grad_att = r.ggat[...] * r.gsig[...]
+    r.gatt[...] = grad_att.astype(BF)
+    r.gt[...] = grad_att.T.astype(BF)
+    r.qt[...] = flip(r.qkv[0])
     sums.ring_relay(1)
     arrived(r.bias.at[pl.ds(0, NS - 1)], r.bs.at[0], r.br.at[0], at)
     wt_copy.wait()
@@ -668,8 +667,9 @@
         grad_s = probs * (grad_probs - delta)
         grad_low = grad_s.astype(BF)
         r.acc[1, :, win] += dot(grad_low, k_m)
-        r.acc[2, :, win] += dot_l(grad_low, q_m)
-        r.acc[3, :, win] += dot_l(low, g_m)
+        own = slice(h * HD, (h + 1) * HD)
+        r.dkt[own] = dot(r.qt[own], grad_low)
+        r.dvt[own] = dot(r.gt[own], low)
         split = grad_s.reshape(NS, 8, N)
         if h % 2 == 0:
             r.held[...] = split
@@ -703,10 +703,10 @@
     r.gheads[:, 1152:] = (r.ggat[...] * attended * r.gsig[...] * (1.0 - r.gsig[...])).astype(BF)
     grad_q = (r.acc[1] * SCALE).astype(BF)
     r.gheads[:, :384] = grad_q
-    r.gheads[:, 384:768] = (r.acc[2] * SCALE).astype(BF)
-    r.gheads[:, 768:1152] = r.acc[3].astype(BF)
+    r.gheads[:, 384:768] = (r.dkt[...].T * SCALE).astype(BF)
+    r.gheads[:, 768:1152] = r.dvt[...].T.astype(BF)
     for j in range(3):
-        r.small_w[9 + j : 10 + j] = jnp.sum(
+        r.small[9 + j : 10 + j] = jnp.sum(
             grad_q[:, j * 128 : (j + 1) * 128].astype(F32), 0, keepdims=True
         )
     for b in blocks:
@@ -735,17 +735,11 @@
     act_copy = rcopy(r.acts, r.actr, r.hs.at[2], r.hr.at[2], head_dev(at))
     act_copy.start()
     conditioned(0, r.tiles[4])
-    conditioning_back(0)
-    r.tiles[4][T_SMALL:T_APAD] = r.small_a[...].astype(BF).reshape(2, 16, 128)
     r.tiles[4][T_APAD:] = jnp.zeros((TILES[4] - T_APAD, 16, 128), BF)
     sums.core_start(4)
     sums.core_end(3)
     for g in (5, 6):
         sums.ring_start(g)
-    grad_single = norm_back(r.gsh[...], r.shat[...], r.sinv[:, :1]) + r.zterm[...]
-    put(r.tiles[5], 0, grad_single)
-    r.tiles[5][48:] = jnp.zeros((TILES[5] - 48, 16, 128), BF)
-    sums.ring_start(10)
     for g in (2, 3, 4):
         sums.gather_start(g)
     for g in (0, 1):
@@ -753,6 +747,12 @@
     sums.core_end(4)
     for g in (7, 8, 9):
         sums.ring_start(g)
+    conditioning_back(1)
+    conditioning_back(0)
+    grad_single = norm_back(r.gsh[...], r.shat[...], r.sinv[:, :1]) + r.zterm[...]
+    put(r.tiles[5], 0, grad_single)
+    r.tiles[5][48:] = jnp.zeros((TILES[5] - 48, 16, 128), BF)
+    sums.ring_start(10)
     for half in range(2):
         arrived(r.gb1.at[half], r.b1s.at[half], r.b1r.at[half], at)
         own = pl.ds(at["zx"[half]] * 8, 8)
@@ -769,7 +769,7 @@
                 r.b2r.at[half],
                 dev,
             ).start()
-    for g in (5, 6, 10):
+    for g in (5, 6):
         sums.ring_relay(g)
     for g in (2, 3, 4):
         sums.gather_ring(g)
@@ -777,6 +777,7 @@
         sums.ring_relay(g)
     for g in (0, 1):
         sums.gather_relay(g)
+    sums.ring_relay(10)
     places = (at["z"] * 8 + at["l"] * 4 + at["x"], at["x"] * 8 + at["z"] * 2 + at["l"])
     for half in range(2):
         arrived(r.gb2.at[half], r.b2s.at[half], r.b2r.at[half], at)
@@ -817,23 +818,29 @@
         total = total + jnp.sum(grad_low * normed, 0, keepdims=True)
         r.gpair[i] = norm_back(grad_low * pgain, normed, inv)
     leave(r.gpair, "pair_o")
-    r.small_w[:8] = weight
-    r.small_w[8:9] = total
+    r.small[:8] = weight
+    r.small[8:9] = total
 
     def small_start(k):
-        axis = "czxl"[k]
+        axis = "czxlh"[k]
         mine = at[axis]
-        r.slot[k, mine] = r.small_w[...]
+        first = 16 if axis == "h" else 0
+        r.slot[k, mine] = r.small[...]
+        rows = r.slot.at[k, mine, pl.ds(first, 48 - first)]
         for i in range(1, SIZE.get(axis, 2)):
-            dev = core_dev(at) if axis == "c" else peer_on(at, axis, i)[0]
-            rcopy(r.slot.at[k, mine], r.slot.at[k, mine], r.ss.at[k], r.sr.at[k], dev).start()
+            dev = {"c": core_dev, "h": head_dev}.get(axis, lambda a: peer_on(a, axis, i)[0])(at)
+            rcopy(rows, rows, r.ss.at[k], r.sr.at[k], dev).start()
 
     def small_end(k):
-        arrived(r.slot.at[k, pl.ds(0, SIZE.get("czxl"[k], 2) - 1)], r.ss.at[k], r.sr.at[k], at)
-        total = r.slot[k, 0]
-        for i in range(1, SIZE.get("czxl"[k], 2)):
-            total = total + r.slot[k, i]
-        r.small_w[...] = total
+        axis = "czxlh"[k]
+        first = 16 if axis == "h" else 0
+        count = SIZE.get(axis, 2)
+        like = r.slot.at[k, pl.ds(0, count - 1), pl.ds(first, 48 - first)]
+        arrived(like, r.ss.at[k], r.sr.at[k], at)
+        total = r.slot[k, 0, first:]
+        for i in range(1, count):
+            total = total + r.slot[k, i, first:]
+        r.small[first:] = total
 
     small_start(0)
     for g in FIRST:
@@ -864,9 +871,11 @@
     for g in SECOND:
         sums.gather_relay(g)
     small_end(3)
-    leave(r.small_w, "small_o")
+    small_start(4)
     for g in SECOND:
         sums.gather_end(g)
+    small_end(4)
+    leave(r.small, "small_o")
     leave(r.sums[5], "sum5")
     own = [pl.ds(sums.shift[b], HALF[b]) for b in range(5)]
     other = [pl.ds((1 - at["c"]) * HALF[b], HALF[b]) for b in range(5)]
@@ -937,14 +946,18 @@
     in_sem, out_sem = take(2)
     loads = []
     for i in range(10):
-        cp = pltpu.make_async_copy(ins[i], held[i], in_sem.at[i])
-        cp.start()
-        loads.append(cp)
+        loads.append(pltpu.make_async_copy(ins[i], held[i], in_sem.at[i]))
+    for i in (2, 4, 0, 3, 1, 5, 6, 7, 8, 9):
+        loads[i].start()
     copies = []
 
-    def leave(name):
+    def leave(name, half=None):
         i = [k for k, _ in FINAL].index(name)
-        cp = pltpu.make_async_copy(getattr(f, name), outs[3 + i], out_sem.at[3 + i])
+        src, dst = getattr(f, name), outs[3 + i]
+        if half is not None:
+            rows = pl.ds(half * 384, 384)
+            src, dst = src.at[rows], dst.at[rows]
+        cp = pltpu.make_async_copy(src, dst, out_sem.at[len(copies)])
         cp.start()
         copies.append(cp)
 
@@ -952,34 +965,6 @@
         return held[b][pl.ds(start, rows // 16)].astype(F32).reshape(rows, 128)
 
     cols = [slice(j * 128, (j + 1) * 128) for j in range(12)]
-    for i in range(3):
-        loads[7 + i].wait()
-        cp = pltpu.make_async_copy(held[7 + i], outs[i], out_sem.at[i])
-        cp.start()
-        copies.append(cp)
-    loads[0].wait()
-    for j in range(6):
-        f.hid[:, cols[j]] = get(0, T_HID + j * 48, 768)
-    leave("hid")
-    loads[3].wait()
-    for k in range(4):
-        for j in range(3):
-            f.qkvg[:, k, cols[j]] = get(3, T_QKVG + (k * 3 + j) * 48, 768)
-    leave("qkvg")
-    for j in range(6):
-        f.wout[:, cols[j]] = get(3, T_OUT + j * 24, 384)
-    leave("wout")
-    loads[1].wait()
-    for i in range(12):
-        k, j = i // 6, i % 6
-        if i < 2:
-            f.win[:, k, cols[j]] = get(0, T_IN0 + i * 48, 768)
-        elif i < 11:
-            f.win[:, k, cols[j]] = get(1, T_IN + (i - 2) * 48, 768)
-        else:
-            f.win[:256, k, cols[j]] = get(1, T_IN + 432, 256)
-            f.win[256:, k, cols[j]] = get(3, T_IN2, 512)
-    leave("win")
     loads[2].wait()
     loads[4].wait()
     for w in range(2):
@@ -993,18 +978,52 @@
             else:
                 f.zero[w, :, cols[j]] = get(4 - 2 * w, T_ZERO[w] + j * 24, 384)
     leave("zero")
+    loads[0].wait()
+    for j in range(6):
+        f.hid[:, cols[j]] = get(0, T_HID + j * 48, 768)
+    leave("hid")
+    loads[3].wait()
+    for c in range(2):
+        for k in range(4):
+            for j in range(3):
+                f.qkvg[c * 384 : c * 384 + 384, k, cols[j]] = get(
+                    3, T_QKVG + (k * 3 + j) * 48 + c * 24, 384
+                )
+        leave("qkvg", c)
+    for j in range(6):
+        f.wout[:, cols[j]] = get(3, T_OUT + j * 24, 384)
+    leave("wout")
+    loads[1].wait()
+    for c in range(2):
+        for i in range(12):
+            k, j = i // 6, i % 6
+            if i < 2:
+                value = get(0, T_IN0 + i * 48 + c * 24, 384)
+            elif i < 11:
+                value = get(1, T_IN + (i - 2) * 48 + c * 24, 384)
+            elif c == 0:
+                value = jnp.concatenate([get(1, T_IN + 432, 256), get(3, T_IN2, 128)], 0)
+            else:
+                value = get(3, T_IN2 + 8, 384)
+            f.win[c * 384 : c * 384 + 384, k, cols[j]] = value
+        leave("win", c)
+    for i in range(3):
+        loads[7 + i].wait()
+        cp = pltpu.make_async_copy(held[7 + i], outs[i], out_sem.at[len(copies)])
+        cp.start()
+        copies.append(cp)
     loads[5].wait()
     for j in range(3):
         f.single[:, cols[j]] = get(5, j * 16, 256)
     leave("single")
-    small = held[4][T_SMALL:T_APAD].astype(F32).reshape(32, 128)
+    loads[6].wait()
+    small = held[6][16:]
     for w in range(2):
         for j in range(6):
             f.adab[w : w + 1, cols[j]] = small[6 * w + j : 6 * w + j + 1]
             f.zerob[w : w + 1, cols[j]] = small[12 + 6 * w + j : 13 + 6 * w + j]
         for j in range(3):
             f.gain[w : w + 1, cols[j]] = small[24 + 3 * w + j : 25 + 3 * w + j]
-    loads[6].wait()
     f.wt[...] = held[6][:8]
     f.pgain[...] = held[6][8]
     for j in range(3):
@@ -1025,7 +1044,7 @@
         out_specs=[pl.BlockSpec(memory_space=pl.ANY)] * len(shapes),
         scratch_shapes=[pltpu.VMEM(a.shape, a.dtype) for a in args]
         + [pltpu.VMEM(shape, F32) for _, shape in FINAL]
-        + [pltpu.SemaphoreType.DMA((10,)), pltpu.SemaphoreType.DMA((len(shapes),))],
+        + [pltpu.SemaphoreType.DMA((10,)), pltpu.SemaphoreType.DMA((len(shapes) + 2,))],
         compiler_params=pltpu.CompilerParams(vmem_limit_bytes=63 * 2**20),
         name="finish",
     )(*args)

time: 128 us -> 123 us (0.961)
  Pallas kernels: 122 us -> 116 us
    pallas_call x1, Pallas kernels: 14.7 us -> 11.2 us  [finish(): pl.pallas_call(finish_kernel, out_shape=tuple(shapes), in_specs=[pl.Block...]
    pallas_call x1, Pallas kernels: 107 us -> 105 us  [mega(): pl.pallas_call(mega_kernel, out_shape=tuple((whole(shape, dtype) for _, s...]
where the time goes in v4:
time: 123 us
  Pallas kernels  116 us (94%)
  local copies, waits for them, and re-layouts  5.23 us (4%)
  between operations  1.49 us (1%)
    pallas_call x1, Pallas kernels, mega(): pl.pallas_call(mega_kernel, out_shape=tuple((whole(shape, dtype) for _, s...  105 us
    pallas_call x1, Pallas kernels, finish(): pl.pallas_call(finish_kernel, out_shape=tuple(shapes), in_specs=[pl.Block...  11.2 us
    unnamed x4, local copies, waits for them, and re-layouts  5.23 us

profile of v4, /device:TPU:1, one launch (start us, length us, event | category | flops | bytes accessed | tf_op | source)
XLA Modules:
  0.0 123.1 jit_solution(843126193639646183)
XLA Ops:
  1.3 0.0 copy-start
  1.3 3.5 %copy.37 = bf16[768,4,384]{2,0,1:T(8,128)(2,1)} copy(bf16[768,4,384]{2,1,0:T(4,128)(2,1)} %param.26) | data formatting | bytes 4718592 | tf_op args[9]
  4.8 0.0 copy-done
  4.8 1.7 %copy.38 = bf16[768,2,768]{2,0,1:T(8,128)(2,1)} copy(bf16[768,2,768]{2,1,0:T(2,128)(2,1)S(1)} %copy-done) | data formatting | bytes 4718592 | tf_op args[12]
  6.5 105.2 %block.1 = (bf16[384,16,128]{2,1,0:T(8,128)(2,1)}, bf16[448,16,128]{2,1,0:T(8,128)(2,1)}, bf16[384,16,128]{2,1,0:T(8,128)(2,1)}, bf16[768,16,128]{2,1,0:T(8,128)...) custom-call(s32[1]{0:T(128)S(6)} %copy.39.refs_0_, ...), custom_call_target="tpu_custom_call" | custom-call | tf_op jit(solution)/shard_map/block/pallas_call | solution.py:896
  111.7 11.2 %finish.1 = (bf16[256,768]{1,0:T(8,128)(2,1)}, f32[256,768]{1,0:T(8,128)}, f32[8,256,128]{2,1,0:T(8,128)}, f32[768,4,384]{2,1,0:T(4,128)}, f32[768,2,768]{2,1,0:...) custom-call(bf16[384,16,128]{2,1,0:T(8,128)(2,1)} %get-tuple-element, ...), custom_call_target="tpu_custom_call" | custom-call | tf_op jit(solution)/shard_map/finish/pallas_call | solution.py:1040
Async XLA Ops:
  1.3 3.5 %copy-start = (bf16[768,2,768]{2,1,0:T(2,128)(2,1)S(1)}, bf16[768,2,768]{2,1,0:T(2,128)(2,1)}, u32[]{:S(2)}) copy-start(bf16[768,2,768]{2,1,0:T(2,128)(2,1)} %param.29) | copy-start | bytes 7077892

commit v5 on v4

--- a/solution.py
+++ b/solution.py
@@ -191,8 +191,7 @@
 N = 256
 SCRATCH = (
     ("rows", (8, 8, N), F32),
-    ("part", (64, N), BF),
-    ("bias", (NS, 64, N), BF),
+    ("bias", (2, NS, 32, N), BF),
     ("wall", (2, 16, 128), BF),
     ("shat", (N, 384), F32),
     ("sinv", (N, 128), F32),
@@ -241,8 +240,8 @@
 )
 SEMS = (
     ("ld", (len(LOADS),)),
-    ("bs", (1,)),
-    ("br", (1,)),
+    ("bs", (4,)),
+    ("br", (4,)),
     ("hs", (4,)),
     ("hr", (4,)),
     ("cs", (5,)),
@@ -455,9 +454,9 @@
         signal(bar, dev)
     blocks = [slice(i * 256, (i + 1) * 256) for i in range(3)]
     loads = {}
-    places = {name: i for i, (name, _) in enumerate(INPUTS)}
+    index = {name: i for i, (name, _) in enumerate(INPUTS)}
     for k, name in enumerate(LOADS):
-        src, dst = hbm[places[name.rstrip("01")]], getattr(r, name.rstrip("01"))
+        src, dst = hbm[index[name.rstrip("01")]], getattr(r, name.rstrip("01"))
         if name[-1] in "01":
             src, dst = src.at[int(name[-1])], dst.at[int(name[-1])]
         cp = pltpu.make_async_copy(src, dst, r.ld.at[k])
@@ -483,16 +482,28 @@
     for i in range(8):
         normed, _ = normalize(r.pair[i].astype(F32))
         r.rows[:, i, :] = dot_t(wt, (normed * pgain).astype(BF))
-    r.part[...] = r.rows[...].reshape(64, N).astype(BF)
-    r.bias[me] = r.part[...]
+    places = (at["z"] * 8 + at["l"] * 4 + at["x"], at["x"] * 8 + at["z"] * 2 + at["l"])
+    part = r.rows[...].reshape(64, N).astype(BF)
+    for half in range(2):
+        r.bias[half, places[half]] = part[half * 32 : half * 32 + 32]
     pl.semaphore_wait(bar, NS + 2)
 
-    def bias_copy(i):
-        return rcopy(
-            r.part, r.bias.at[me], r.bs.at[0], r.br.at[0], samp_dev(at, (me + i) % NS)
-        )
-
-    loop(NS - 1, lambda i: bias_copy(i + 1).start())
+    def bias_send(half, hop):
+        if hop == 0:
+            rows, axes = pl.ds(places[half], 1), ("lx", "zl")[half]
+        else:
+            rows, axes = pl.ds(at["zx"[half]] * 8, 8), "zx"[half]
+        mine = r.bias.at[half, rows]
+        k = half + 2 * hop
+        for i in range(1, extent(axes)):
+            rcopy(mine, mine, r.bs.at[k], r.br.at[k], peer_on(at, axes, i)[0]).start()
+
+    def bias_wait(half, hop):
+        k = half + 2 * hop
+        arrived(r.bias.at[half, pl.ds(0, (7, 24)[hop])], r.bs.at[k], r.br.at[k], at)
+
+    for half in range(2):
+        bias_send(half, 0)
     wt_copy = rcopy(r.wall.at[hd], r.wall.at[hd], r.hs.at[0], r.hr.at[0], head_dev(at))
     wt_copy.start()
 
@@ -536,6 +547,9 @@
     modulation(1)
     need("act", "cot")
     branch_start(1, r.tin, r.gto)
+    for half in range(2):
+        bias_wait(half, 0)
+        bias_send(half, 1)
 
     def branch_out(w, b, part):
         gate = r.zg[w, :, b]
@@ -639,7 +653,8 @@
     r.gt[...] = grad_att.T.astype(BF)
     r.qt[...] = flip(r.qkv[0])
     sums.ring_relay(1)
-    arrived(r.bias.at[pl.ds(0, NS - 1)], r.bs.at[0], r.br.at[0], at)
+    bias_wait(0, 1)
+    bias_wait(1, 1)
     wt_copy.wait()
     r.acc[...] = jnp.zeros(r.acc.shape, F32)
     lane = lax.broadcasted_iota(jnp.int32, (1, 256), 1)
@@ -654,7 +669,11 @@
         k_m = r.qkv[1, :, win] * pick
         v_m = r.qkv[2, :, win] * pick
         g_m = r.gatt[:, win] * pick
-        pair_rows = r.bias[:, (h // 2) * 16 : (h // 2) * 16 + 16, :].astype(F32)
+        rows = slice((h // 2 % 2) * 16, (h // 2 % 2) * 16 + 16)
+        pair_rows = r.bias[h // 4, :, rows, :].astype(F32)
+        if h >= 4:
+            order = [s % 4 * 8 + s // 8 * 2 + s // 4 % 2 for s in range(NS)]
+            pair_rows = jnp.stack([pair_rows[s] for s in order])
         bias = pair_rows[:, (h % 2) * 8 : (h % 2) * 8 + 8, :].reshape(N, N)
         scores = dot_t(q_m, r.qkv[1, :, win]) * SCALE + bias + mask
         top = jnp.max(scores, -1, keepdims=True)
@@ -778,7 +797,6 @@
     for g in (0, 1):
         sums.gather_relay(g)
     sums.ring_relay(10)
-    places = (at["z"] * 8 + at["l"] * 4 + at["x"], at["x"] * 8 + at["z"] * 2 + at["l"])
     for half in range(2):
         arrived(r.gb2.at[half], r.b2s.at[half], r.b2r.at[half], at)
         total = r.gb[half, places[half]].astype(F32)

time: 123 us -> 121 us (0.984)
  Pallas kernels: 116 us -> 114 us
    pallas_call x1, Pallas kernels: 105 us -> 103 us  [mega(): pl.pallas_call(mega_kernel, out_shape=tuple((whole(shape, dtype) for _, s...]
where the time goes in v5:
time: 121 us
  Pallas kernels  114 us (94%)
  local copies, waits for them, and re-layouts  5.23 us (4%)
  between operations  1.49 us (1%)
    pallas_call x1, Pallas kernels, mega(): pl.pallas_call(mega_kernel, out_shape=tuple((whole(shape, dtype) for _, s...  103 us
    pallas_call x1, Pallas kernels, finish(): pl.pallas_call(finish_kernel, out_shape=tuple(shapes), in_specs=[pl.Block...  11.2 us
    unnamed x4, local copies, waits for them, and re-layouts  5.23 us

profile of v5, /device:TPU:1, one launch (start us, length us, event | category | flops | bytes accessed | tf_op | source)
XLA Modules:
  0.0 121.0 jit_solution(14157205395139991182)
XLA Ops:
  1.3 0.0 copy-start
  1.3 3.5 %copy.37 = bf16[768,4,384]{2,0,1:T(8,128)(2,1)} copy(bf16[768,4,384]{2,1,0:T(4,128)(2,1)} %param.26) | data formatting | bytes 4718592 | tf_op args[9]
  4.8 0.0 copy-done
  4.8 1.7 %copy.38 = bf16[768,2,768]{2,0,1:T(8,128)(2,1)} copy(bf16[768,2,768]{2,1,0:T(2,128)(2,1)S(1)} %copy-done) | data formatting | bytes 4718592 | tf_op args[12]
  6.5 103.1 %block.1 = (bf16[384,16,128]{2,1,0:T(8,128)(2,1)}, bf16[448,16,128]{2,1,0:T(8,128)(2,1)}, bf16[384,16,128]{2,1,0:T(8,128)(2,1)}, bf16[768,16,128]{2,1,0:T(8,128)...) custom-call(s32[1]{0:T(128)S(6)} %copy.39.refs_0_, ...), custom_call_target="tpu_custom_call" | custom-call | tf_op jit(solution)/shard_map/block/pallas_call | solution.py:914
  109.7 11.2 %finish.1 = (bf16[256,768]{1,0:T(8,128)(2,1)}, f32[256,768]{1,0:T(8,128)}, f32[8,256,128]{2,1,0:T(8,128)}, f32[768,4,384]{2,1,0:T(4,128)}, f32[768,2,768]{2,1,0:...) custom-call(bf16[384,16,128]{2,1,0:T(8,128)(2,1)} %get-tuple-element, ...), custom_call_target="tpu_custom_call" | custom-call | tf_op jit(solution)/shard_map/finish/pallas_call | solution.py:1058
Async XLA Ops:
  1.3 3.5 %copy-start = (bf16[768,2,768]{2,1,0:T(2,128)(2,1)S(1)}, bf16[768,2,768]{2,1,0:T(2,128)(2,1)}, u32[]{:S(2)}) copy-start(bf16[768,2,768]{2,1,0:T(2,128)(2,1)} %param.29) | copy-start | bytes 7077892
